TPU v7x, 128 devices: a whole 4x4x4 slice. The times are simulated.
128 devices in a mesh: grp: 4 (over y_lo, core), blk: 32 (over y_hi, z, x).
Axes of the slice: x: 4, y: 4 (y_hi: 2, y_lo: 2; y = y_hi * 2 + y_lo), z: 4, core: 2. Of those that a mesh axis runs over, the one named last changes fastest.
Arguments:
- volume: float32 [256, 768, 768], P(('grp', 'blk')), may hold values from 0 to 2
- voxel_norm: float32 [256, 768, 768], P(('grp', 'blk')), may hold values from 0.6 to 2.4
- measured: float32 [768, 32, 1024], P('grp', 'blk'), may hold values from -6 to 6
- ray_norm: float32 [768, 32, 1024], P('grp', 'blk'), may hold values from 0.5 to 2
- axial_weights: float32 [256, 32, 8], P(('grp', 'blk')), may hold values from 0.05 to 1
- row_start: int32 [32, 128], replicated, may hold values from 0 to 760, as said below
- row_order: int32 [768], replicated, may hold values from 0 to 767, each once
- subset: int32 [32], replicated, may hold values from 0 to 1023
Outputs:
- new_volume: float32 [256, 768, 768], P(('grp', 'blk'))
- residual: float32 [768, 32, 1024], P('grp', 'blk')
Inputs may be any that keep to these rules, and one draw needn't show every extreme that they name: row_start[a, s] rises strictly with s, every footprint lies on the detector, and within each group of 32 consecutive slabs (equal s // 32) a slab's footprint starts at most 155 rows after the group's first slab's; both bounds are reached. `row_order`: a permutation of the detector rows.
All inputs are finite; a program needn't handle non-finite values.
Results may differ from a plain program's by a relative error of at most 0.0015.
Values may be sent and summed in bfloat16 or wider, within the bound.
A program may use at most 128 MiB of HBM per device.

v0:
```python
import math

import jax
import jax.numpy as jnp
from jax import lax
from jax.sharding import PartitionSpec as P

TOTAL_ANG = 1024


precise = lax.Precision.HIGHEST


def view_angles(subset):
    return 2.0 * math.pi / TOTAL_ANG * subset.astype(jnp.float32)


def transaxial_weights(view_angle, detector_cols, volume_cols):
    positions = jnp.arange(volume_cols, dtype=jnp.float32)
    detector_pos = jnp.arange(detector_cols, dtype=jnp.float32)
    centre = (
        (detector_cols - 1) / 2.0
        + 0.8 * detector_cols / volume_cols * (positions - (volume_cols - 1) / 2.0)[None, :]
        + 0.05 * detector_cols * jnp.sin(view_angle)[:, None]
    )
    return jnp.maximum(0.0, 1.0 - jnp.abs(detector_pos[None, :, None] - centre[:, None, :]))


def depth_weights(view_angle, depth_cells):
    positions = jnp.arange(depth_cells, dtype=jnp.float32)
    middle = (depth_cells - 1) / 2.0 * (1.0 + 0.8 * jnp.sin(view_angle))
    bump = jnp.maximum(
        0.0, 1.0 - jnp.abs(positions[None, :] - middle[:, None]) / (0.1 * depth_cells)
    )
    return (1.0 + 2.0 * bump) / depth_cells


def shards(volume, voxel_norm, measured, ray_norm, axial_weights, row_start, row_order, subset):
    members = lax.axis_size("blk")
    groups = lax.axis_size("grp")
    slices, depth_cells, volume_cols = volume.shape
    owned_rows, own_angles, detector_cols = measured.shape
    footprint = axial_weights.shape[2]
    angles = subset.shape[0]
    detector_rows = row_order.shape[0]
    stride_max = (detector_rows - footprint) // (groups * members - 1)
    band_height = footprint + (members - 1) * stride_max
    group_index = lax.axis_index("grp")
    member_index = lax.axis_index("blk")
    slab_index = group_index * members + member_index
    group_first = group_index * members
    view_angle = view_angles(subset)
    depth_weight = depth_weights(view_angle, depth_cells)
    blocks = angles // 8
    summed = jnp.einsum("ay,zyx->azx", depth_weight, volume, precision=precise)

    def project(pieces):
        return jnp.einsum(
            "aux,azx->azu",
            transaxial_weights(pieces[0], detector_cols, volume_cols),
            pieces[1],
            precision=precise,
        )

    sinogram = lax.map(
        project, (view_angle.reshape(blocks, 8), summed.reshape(blocks, 8, slices, volume_cols))
    ).reshape(angles, slices, detector_cols)
    partial_value = jnp.einsum("qar,aqu->aru", axial_weights, sinogram, precision=precise)
    received = lax.all_to_all(
        partial_value.reshape(members, own_angles, footprint, detector_cols),
        "blk",
        split_axis=0,
        concat_axis=0,
        tiled=True,
    )
    my_angles = member_index * own_angles + jnp.arange(own_angles, dtype=jnp.int32)
    starts = lax.dynamic_slice_in_dim(row_start[my_angles], group_first, members, 1)
    band_low = starts[:, 0]
    offsets = starts - band_low[:, None]
    heights = jnp.arange(band_height, dtype=jnp.int32)
    within = jnp.arange(footprint, dtype=jnp.int32)
    placement = (
        heights[None, :, None, None] == offsets[:, None, :, None] + within[None, None, None, :]
    ).astype(jnp.float32)
    band_sums = jnp.einsum("awsr,saru->awu", placement, received, precision=precise)
    local_rows = row_order[:, None] - band_low[None, :]
    select = (local_rows[:, :, None] == heights[None, None, :]).astype(jnp.float32)
    forward_own = lax.psum_scatter(
        jnp.einsum("jaw,awu->jau", select, band_sums, precision=precise),
        "grp",
        scatter_dimension=0,
        tiled=True,
    )
    residual = ray_norm * (measured - forward_own)
    ratio_rows = residual.astype(jnp.bfloat16)
    gathered = lax.all_gather(ratio_rows, "grp", axis=0, tiled=True)
    inverse = (
        jnp.zeros((detector_rows,), jnp.int32)
        .at[row_order]
        .set(jnp.arange(detector_rows, dtype=jnp.int32))
    )
    band_index = inverse[jnp.minimum(band_low[:, None] + heights[None, :], detector_rows - 1)]
    band_ratio = gathered[band_index, jnp.arange(own_angles, dtype=jnp.int32)[:, None], :]
    my_offsets = row_start[:, slab_index] - row_start[:, group_first]

    def take_rows(segment, offset_row):
        return lax.dynamic_slice_in_dim(segment, offset_row, footprint, 0)

    rows_now = jax.vmap(take_rows)(
        lax.all_gather(band_ratio, "blk", axis=0, tiled=True), my_offsets
    ).astype(jnp.float32)
    contributions = jnp.einsum("qar,aru->aqu", axial_weights, rows_now, precision=precise)

    def spread_block(pieces):
        return jnp.einsum(
            "aux,azu->azx",
            transaxial_weights(pieces[0], detector_cols, volume_cols),
            pieces[1],
            precision=precise,
        )

    spread = lax.map(
        spread_block,
        (view_angle.reshape(blocks, 8), contributions.reshape(blocks, 8, slices, detector_cols)),
    ).reshape(angles, slices, volume_cols)
    update = jnp.einsum("ay,azx->zyx", depth_weight, spread, precision=precise)
    return (jnp.maximum(0.0, volume + voxel_norm * update), residual)


def solution(mesh):
    placed = (
        P(("grp", "blk"), None, None),
        P(("grp", "blk"), None, None),
        P("grp", "blk", None),
        P("grp", "blk", None),
        P(("grp", "blk"), None, None),
        P(),
        P(),
        P(),
    )
    return jax.shard_map(
        shards,
        mesh=mesh,
        in_specs=placed,
        out_specs=(P(("grp", "blk"), None, None), P("grp", "blk", None)),
        check_vma=False,
    )
```

profile of v0, /device:TPU:1, one launch (start us, length us, event | category | flops | bytes accessed | tf_op | source)
XLA Modules:
  0.0 558.9 jit_solution(11983078879597247558)
XLA Ops:
  7.2 0.7 convert_multiply_fusion
  7.9 0.1 reshape.244
  8.0 5.1 convolution_bitcast_fusion.3
  13.1 0.0 copy-start.1
  13.1 0.0 copy-start
  13.1 0.0 copy-start.2
  13.1 127.9 %while.25 = (s32[]{:T(128)}, f32[4,8,2,1024]{3,2,1,0:T(2,128)S(1)}, f32[4,8,2,768]{3,1,0,2:T(8,128)S(1)}, f32[4,8]{1,0:T(4,128)S(1)}, s32[]{:T(128)}) while((s32[]{:T(128)}, f32[4,8,2,1024]{3,2,1,0:T(2,128)S(1)}, f32[4,8,2,768]{3,1,0,2:T(8,128)S(1)}, f32[4,8]{1,0:T(4,128)S(1)}, s32[]{:T(128)}) %tuple.65), condition=%wide.region_1.2_spmd, body=%wide.region_0.1_spmd.sunk | while | flops 176169232 | bytes 268457 | solution.py:65
  13.2 0.1 broadcast_add_fusion.4
  13.3 31.8 %fusion.101 = f32[4,8,2,1024]{3,2,1,0:T(2,128)S(1)} fusion(f32[4,8,2,1024]{3,2,1,0:T(2,128)S(1)} %get-tuple-element.217, s32[]{:T(128)} %get-tuple-element.216, f32[8,768]{1,0:T(8,128)S(1)} %broadcast_add_fusion.4, f32[1,8,2,768]{3,1,0,2:T(8,128)S(1)} %constant_dynamic-slice_fusion.4), kind=kOutput, calls=%fused_computation.14.clone.1 | convolution fusion | flops 176160768 | bytes 139268 | tf_op jit(solution)/shard_map/while/body/eval_jaxpr/aux,azx->azu/dot_general | solution.py:58
  45.2 0.1 broadcast_add_fusion.4
  45.3 31.8 %fusion.101 = f32[4,8,2,1024]{3,2,1,0:T(2,128)S(1)} fusion(f32[4,8,2,1024]{3,2,1,0:T(2,128)S(1)} %get-tuple-element.217, s32[]{:T(128)} %get-tuple-element.216, f32[8,768]{1,0:T(8,128)S(1)} %broadcast_add_fusion.4, f32[1,8,2,768]{3,1,0,2:T(8,128)S(1)} %constant_dynamic-slice_fusion.4), kind=kOutput, calls=%fused_computation.14.clone.1 | convolution fusion | flops 176160768 | bytes 139268 | tf_op jit(solution)/shard_map/while/body/eval_jaxpr/aux,azx->azu/dot_general | solution.py:58
  77.2 0.1 broadcast_add_fusion.4
  77.3 31.8 %fusion.101 = f32[4,8,2,1024]{3,2,1,0:T(2,128)S(1)} fusion(f32[4,8,2,1024]{3,2,1,0:T(2,128)S(1)} %get-tuple-element.217, s32[]{:T(128)} %get-tuple-element.216, f32[8,768]{1,0:T(8,128)S(1)} %broadcast_add_fusion.4, f32[1,8,2,768]{3,1,0,2:T(8,128)S(1)} %constant_dynamic-slice_fusion.4), kind=kOutput, calls=%fused_computation.14.clone.1 | convolution fusion | flops 176160768 | bytes 139268 | tf_op jit(solution)/shard_map/while/body/eval_jaxpr/aux,azx->azu/dot_general | solution.py:58
  109.2 0.1 broadcast_add_fusion.4
  109.2 31.8 %fusion.101 = f32[4,8,2,1024]{3,2,1,0:T(2,128)S(1)} fusion(f32[4,8,2,1024]{3,2,1,0:T(2,128)S(1)} %get-tuple-element.217, s32[]{:T(128)} %get-tuple-element.216, f32[8,768]{1,0:T(8,128)S(1)} %broadcast_add_fusion.4, f32[1,8,2,768]{3,1,0,2:T(8,128)S(1)} %constant_dynamic-slice_fusion.4), kind=kOutput, calls=%fused_computation.14.clone.1 | convolution fusion | flops 176160768 | bytes 139268 | tf_op jit(solution)/shard_map/while/body/eval_jaxpr/aux,azx->azu/dot_general | solution.py:58
  141.0 0.0 copy-done.1
  141.1 0.1 copy.37
  141.2 2.1 convolution_bitcast_fusion.1
  143.2 11.3 %all-to-all-start = ((f32[32,1,8,1024]{3,2,1,0:T(8,128)}), f32[32,1,8,1024]{3,2,1,0:T(8,128)S(1)}, u32[]{:S(2)}, u32[]{:S(2)}) async-start(f32[32,1,8,1024]{3,2,1,0:T(8,128)} %convolution_bitcast_fusion.1), calls=%async_computation | async-start | bytes 2097152 | tf_op jit(solution)/shard_map/all_to_all | solution.py:69
  154.6 0.0 all-reduce.5.cloned.1.call-start
  154.6 0.0 copy-done
  154.6 0.1 dynamic_slice.36
  154.7 0.1 subtract_bitcast_fusion
  154.8 0.0 copy-done.2
  154.9 0.1 iota_add_fusion
  154.9 16.5 %all-to-all-done = f32[32,1,8,1024]{3,2,1,0:T(8,128)S(1)} async-done(((f32[32,1,8,1024]{3,2,1,0:T(8,128)}), f32[32,1,8,1024]{3,2,1,0:T(8,128)S(1)}, u32[]{:S(2)}, u32[]{:S(2)}) %all-to-all-start) | async-done | bytes 1048608 | tf_op jit(solution)/shard_map/all_to_all | solution.py:69
  171.5 0.6 convolution_bitcast_fusion.2
  172.1 2.8 convolution_bitcast_fusion
  174.9 0.0 copy-start.3
  174.9 5.3 copy.39
  180.2 0.0 all-reduce.5.cloned.1.call-update
  180.2 0.0 all-gather.5.cloned.1.call-start
  180.3 0.0 copy-done.3
  180.3 0.6 dynamic-slice.4
  181.5 71.5 %all-reduce.5.cloned.1.call-done = f32[768,1,1024]{2,1,0:T(1,128)} async-done(((f32[768,1,1024]{2,1,0:T(1,128)}), f32[768,1,1024]{2,1,0:T(1,128)}) %all-reduce.5.cloned.1.call-update) | async-done | bytes 3145744
  253.0 3.8 fusion.85
  256.8 0.9 copy.40
  257.7 0.0 all-gather.5.cloned.1.call-update
  257.7 0.0 all-gather.7.cloned.1.call-start
  257.8 3.6 scatter_custom_fusion
  261.4 1.2 gather_fusion
  262.6 21.1 %all-gather.5.cloned.1.call-done = bf16[768,1,1024]{2,0,1:T(8,128)(2,1)} async-done(((bf16[192,1,1024]{2,0,1:T(8,128)(2,1)}), bf16[768,1,1024]{2,0,1:T(8,128)(2,1)}) %all-gather.5.cloned.1.call-update) | async-done | bytes 1572880 | tf_op jit(solution)/shard_map/all_gather | solution.py:96
  283.7 7.0 %gather_fusion.1 = bf16[163,1024]{1,0:T(8,128)(2,1)} fusion(bf16[768,1,1024]{2,0,1:T(8,128)(2,1)} %all-gather.5.cloned.1.call-done, s32[163]{0:T(256)S(1)} %bitcast.81), kind=kCustom, calls=%fused_computation.1 | custom fusion | bytes 668952 | tf_op jit(solution)/shard_map/gather | solution.py:103
  290.7 0.0 all-gather.7.cloned.1.call-update
  290.7 6.0 %copy.46 = f32[2,768,768]{1,2,0:T(8,128)} copy(f32[2,768,768]{2,1,0:T(8,128)} %param.12) | data formatting | bytes 9437184 | tf_op args[0]
  296.8 6.1 %copy.45 = f32[2,768,768]{1,2,0:T(8,128)} copy(f32[2,768,768]{2,1,0:T(8,128)} %param.13) | data formatting | bytes 9437184 | tf_op args[1]
  302.9 0.2 fusion.69
  303.1 107.4 %all-gather.7.cloned.1.call-done = bf16[32,163,1024]{2,1,0:T(8,128)(2,1)} async-done(((bf16[1,163,1024]{2,1,0:T(8,128)(2,1)}), bf16[32,163,1024]{2,1,0:T(8,128)(2,1)}) %all-gather.7.cloned.1.call-update) | async-done | bytes 10682384 | tf_op jit(solution)/shard_map/all_gather | solution.py:110
  410.4 23.2 %copy.41 = bf16[32,163,1024]{2,0,1:T(8,128)(2,1)} copy(bf16[32,163,1024]{2,1,0:T(8,128)(2,1)} %all-gather.7.cloned.1.call-done) | data formatting | bytes 21364736 | tf_op jit(solution)/shard_map/all_gather | solution.py:110
  433.6 2.7 gather_fusion.2
  436.3 0.7 fusion.47
  437.1 100.7 %while.26 = (s32[]{:T(128)}, f32[4,8,2,768]{3,2,1,0:T(2,128)S(1)}, f32[4,8,2,1024]{3,2,1,0:T(2,128)S(1)}, f32[4,8]{1,0:T(4,128)S(1)}, s32[]{:T(128)}) while((s32[]{:T(128)}, f32[4,8,2,768]{3,2,1,0:T(2,128)S(1)}, f32[4,8,2,1024]{3,2,1,0:T(2,128)S(1)}, f32[4,8]{1,0:T(4,128)S(1)}, s32[]{:T(128)}) %tuple.78), condition=%wide.region_5.6_spmd, body=%wide.region_4.5_spmd.sunk | while | flops 176169232 | bytes 171169 | solution.py:122
  437.1 0.1 broadcast_add_fusion.5
  437.2 25.0 %fusion.105 = f32[4,8,2,768]{3,2,1,0:T(2,128)S(1)} fusion(f32[4,8,2,768]{3,2,1,0:T(2,128)S(1)} %get-tuple-element.232, s32[]{:T(128)} %get-tuple-element.231, f32[8,768]{1,0:T(8,128)S(1)} %broadcast_add_fusion.5, f32[4,8,2,1024]{3,2,1,0:T(2,128)S(1)} %get-tuple-element.238), kind=kOutput, calls=%fused_computation.35.clone.1 | convolution fusion | flops 176160768 | bytes 140288 | tf_op jit(solution)/shard_map/while/body/eval_jaxpr/aux,azu->azx/dot_general | solution.py:115
  462.3 0.1 broadcast_add_fusion.5
  462.4 25.0 %fusion.105 = f32[4,8,2,768]{3,2,1,0:T(2,128)S(1)} fusion(f32[4,8,2,768]{3,2,1,0:T(2,128)S(1)} %get-tuple-element.232, s32[]{:T(128)} %get-tuple-element.231, f32[8,768]{1,0:T(8,128)S(1)} %broadcast_add_fusion.5, f32[4,8,2,1024]{3,2,1,0:T(2,128)S(1)} %get-tuple-element.238), kind=kOutput, calls=%fused_computation.35.clone.1 | convolution fusion | flops 176160768 | bytes 140288 | tf_op jit(solution)/shard_map/while/body/eval_jaxpr/aux,azu->azx/dot_general | solution.py:115
  487.5 0.1 broadcast_add_fusion.5
  487.6 25.0 %fusion.105 = f32[4,8,2,768]{3,2,1,0:T(2,128)S(1)} fusion(f32[4,8,2,768]{3,2,1,0:T(2,128)S(1)} %get-tuple-element.232, s32[]{:T(128)} %get-tuple-element.231, f32[8,768]{1,0:T(8,128)S(1)} %broadcast_add_fusion.5, f32[4,8,2,1024]{3,2,1,0:T(2,128)S(1)} %get-tuple-element.238), kind=kOutput, calls=%fused_computation.35.clone.1 | convolution fusion | flops 176160768 | bytes 140288 | tf_op jit(solution)/shard_map/while/body/eval_jaxpr/aux,azu->azx/dot_general | solution.py:115
  512.7 0.1 broadcast_add_fusion.5
  512.8 25.0 %fusion.105 = f32[4,8,2,768]{3,2,1,0:T(2,128)S(1)} fusion(f32[4,8,2,768]{3,2,1,0:T(2,128)S(1)} %get-tuple-element.232, s32[]{:T(128)} %get-tuple-element.231, f32[8,768]{1,0:T(8,128)S(1)} %broadcast_add_fusion.5, f32[4,8,2,1024]{3,2,1,0:T(2,128)S(1)} %get-tuple-element.238), kind=kOutput, calls=%fused_computation.35.clone.1 | convolution fusion | flops 176160768 | bytes 140288 | tf_op jit(solution)/shard_map/while/body/eval_jaxpr/aux,azu->azx/dot_general | solution.py:115
  537.8 8.5 %fusion.44 = f32[2,768,768]{1,2,0:T(8,128)} fusion(f32[2,768,768]{1,2,0:T(8,128)} %copy.46, f32[2,768,768]{1,2,0:T(8,128)} %copy.45, f32[32,2,768]{2,1,0:T(2,128)S(1)} %bitcast.85, f32[32]{0:T(128)S(1)} %get-tuple-element.160), kind=kOutput, calls=%fused_computation.49 | convolution fusion | flops 456720384 | bytes 14352512 | tf_op jit(solution)/shard_map/ay,azx->zyx/dot_general | solution.py:126
  546.3 6.0 %copy.47 = f32[2,768,768]{2,1,0:T(8,128)} copy(f32[2,768,768]{1,2,0:T(8,128)} %fusion.44) | data formatting | bytes 9437184
  (29 shorter events, 0.6 us)
Async XLA Ops:
  13.1 127.9 %copy-start.1 = (f32[2,32,8]{1,2,0:T(8,128)S(1)}, f32[2,32,8]{1,2,0:T(8,128)}, u32[]{:S(2)}) copy-start(f32[2,32,8]{1,2,0:T(8,128)} %param.16) | copy-start | bytes 6148
  13.1 141.5 %copy-start = (s32[32,128]{1,0:T(8,128)S(1)}, s32[32,128]{1,0:T(8,128)}, u32[]{:S(2)}) copy-start(s32[32,128]{1,0:T(8,128)} %param.17) | copy-start | bytes 49156
  13.1 141.7 %copy-start.2 = (s32[768]{0:T(1024)S(1)}, s32[768]{0:T(1024)}, u32[]{:S(2)}) copy-start(s32[768]{0:T(1024)} %param.18) | copy-start | bytes 9220
  143.2 28.3 %all-to-all-start = ((f32[32,1,8,1024]{3,2,1,0:T(8,128)}), f32[32,1,8,1024]{3,2,1,0:T(8,128)S(1)}, u32[]{:S(2)}, u32[]{:S(2)}) async-start(f32[32,1,8,1024]{3,2,1,0:T(8,128)} %convolution_bitcast_fusion.1), calls=%async_computation | async-start | bytes 2097152 | tf_op jit(solution)/shard_map/all_to_all | solution.py:69
  154.6 98.4 %all-reduce.5.cloned.1.call-start = ((), (), s32[]{:S(2)}) async-start(), calls=%async_computation.3 | async-start | bytes 6291456
  174.9 5.4 copy-start.3
  180.2 103.5 %all-gather.5.cloned.1.call-start = ((), (), s32[]{:S(2)}) async-start(), calls=%async_computation.1 | async-start | bytes 1966080 | tf_op jit(solution)/shard_map/all_gather | solution.py:96
  257.7 152.7 %all-gather.7.cloned.1.call-start = ((), (), s32[]{:S(2)}) async-start(), calls=%async_computation.2 | async-start | bytes 11354112 | tf_op jit(solution)/shard_map/all_gather | solution.py:110
Sparse Core Ops, SparseCore 0:
  180.4 72.5 all-reduce.4
  257.9 25.7 all-gather.4
  290.8 119.5 all-gather.6
where the time goes:
time: 560 us; the launch traced here: 559 us
  matrix products  247 us (44%)
  waiting for transfers between devices  216 us (39%)
  local copies, waits for them, and re-layouts  62.9 us (11%)
  between operations  14.6 us (3%)
  starting transfers between devices  11.5 us (2%)
  other arithmetic  6.05 us (1%)
    dot_general x4, matrix products, project(): jnp.einsum('aux,azx->azu', transaxial_weights(pieces[0], detector_cols, v...  127 us
    all_gather x1, waiting for transfers between devices, shards(): lax.all_gather(band_ratio, 'blk', axis=0, tiled=True)  107 us
    dot_general x4, matrix products, spread_block(): jnp.einsum('aux,azu->azx', transaxial_weights(pieces[0], detector_cols, v...  100 us
    unnamed x4, waiting for transfers between devices  71.5 us
    all_gather x1, local copies, waits for them, and re-layouts, shards(): lax.all_gather(band_ratio, 'blk', axis=0, tiled=True)  23.2 us
    all_gather x1, waiting for transfers between devices, shards(): gathered = lax.all_gather(ratio_rows, 'grp', axis=0, tiled=True)  21.1 us
    unnamed x13, local copies, waits for them, and re-layouts  18.9 us
    all_to_all x1, waiting for transfers between devices, shards(): lax.all_to_all(partial_value.reshape(members, own_angles, footprint, dete...  16.5 us
  transfers between devices with their start and end apart: 4, of which 4 were waited for; matrix products, arithmetic and copies ran while one was open for 3% of the time, Pallas kernels for 0%

commit v1 on v0

v1 whole, which is shorter than its diff:
```python
import functools
import math

import jax
import jax.numpy as jnp
from jax import lax
from jax.experimental import pallas as pl
from jax.experimental.pallas import tpu as pltpu
from jax.sharding import PartitionSpec as P

TOTAL_ANG = 1024
MESH = pl.DeviceIdType.MESH
LANES = 128
ANGLES = 32
FOOT = 8
COLS = 768
DEPTH = 768
CELLS = 1024
ROWS = 192
STEP = 0.8 * CELLS / COLS


def halves(value):
    high = value.astype(jnp.bfloat16)
    return high, (value - high.astype(jnp.float32)).astype(jnp.bfloat16)


def dot(left, right):
    return jnp.dot(left, right, preferred_element_type=jnp.float32)


def depth_weight(cell, sine):
    middle = (DEPTH - 1) / 2.0 * (1.0 + 0.8 * sine)
    bump = jnp.maximum(0.0, 1.0 - jnp.abs(cell - middle) / (0.1 * DEPTH))
    return (1.0 + 2.0 * bump) / DEPTH


def centre_of(col, shift):
    return ((CELLS - 1) / 2.0 + STEP * (col - (COLS - 1) / 2.0)) + shift


def pick(tiles, first, last, index):
    inside = index & (LANES - 1)
    tile = index >> 7
    value = None
    for number in range(first, last + 1):
        found = jnp.take_along_axis(tiles[number], inside, axis=1, mode="promise_in_bounds")
        value = found if value is None else jnp.where(tile == number, found, value)
    return value


def span(low, high, tiles):
    first = max(0, min(tiles - 1, math.floor(low) // LANES))
    return first, max(first, min(tiles - 1, math.floor(high) // LANES))


def forward_kernel(sine_ref, volume_ref, out_ref, total):
    slice_index, part = pl.program_id(0), pl.program_id(1)
    block = volume_ref.shape[1]
    cell = (lax.broadcasted_iota(jnp.int32, (ANGLES, block), 1) + part * block).astype(jnp.float32)
    high, low = halves(depth_weight(cell, sine_ref[:, :1]))
    volume_high, volume_low = halves(volume_ref[0])
    both = dot(jnp.concatenate([high, low], axis=0), volume_high)
    piece = both[:ANGLES] + (both[ANGLES:] + dot(high, volume_low))

    @pl.when(part == 0)
    def _():
        total[...] = piece

    @pl.when(part > 0)
    def _():
        total[...] += piece

    @pl.when(part == pl.num_programs(1) - 1)
    def _():
        shift = (0.05 * CELLS) * sine_ref[...]
        tiles = [total[:, t * LANES:(t + 1) * LANES] for t in range(COLS // LANES)]
        lane = lax.broadcasted_iota(jnp.int32, (ANGLES, LANES), 1).astype(jnp.float32)
        for chunk in range(CELLS // LANES):
            detector = lane + chunk * LANES
            nearest = jnp.floor((detector - (CELLS - 1) / 2.0 - shift) * (1.0 / STEP) + (COLS - 1) / 2.0)
            middle = (chunk * LANES - (CELLS - 1) / 2.0) / STEP + (COLS - 1) / 2.0
            first, last = span(middle - 49.5, middle + 49.5 + 128 / STEP + 1, COLS // LANES)
            value = None
            for near in (0.0, 1.0):
                col = nearest + near
                weight = jnp.maximum(0.0, 1.0 - jnp.abs(detector - centre_of(col, shift)))
                weight = jnp.where((col >= 0.0) & (col <= COLS - 1.0), weight, 0.0)
                term = weight * pick(tiles, first, last, col.astype(jnp.int32))
                value = term if value is None else value + term
            out_ref[pl.ds(slice_index * 8 + chunk, ANGLES, stride=16), :] = value


def final_kernel(sine_ref, row_ref, back_ref, volume_ref, norm_ref, out_ref, spread):
    slice_index, part = pl.program_id(0), pl.program_id(1)
    block = volume_ref.shape[1]

    @pl.when(part == 0)
    def _():
        shift = (0.05 * CELLS) * sine_ref[...]
        tiles = [
            back_ref[pl.ds(slice_index * 8 + chunk, ANGLES, stride=16), :]
            for chunk in range(CELLS // LANES)
        ]
        lane = lax.broadcasted_iota(jnp.int32, (ANGLES, LANES), 1).astype(jnp.float32)
        for chunk in range(COLS // LANES):
            centre = centre_of(lane + chunk * LANES, shift)
            left = jnp.floor(centre)
            middle = (CELLS - 1) / 2.0 + STEP * (chunk * LANES - (COLS - 1) / 2.0)
            first, last = span(middle - 52.5, middle + 52.5 + STEP * 128 + 1, CELLS // LANES)
            value = None
            for near in (0.0, 1.0):
                detector = left + near
                weight = jnp.maximum(0.0, 1.0 - jnp.abs(detector - centre))
                term = weight * pick(tiles, first, last, detector.astype(jnp.int32))
                value = term if value is None else value + term
            high, low = halves(value)
            here = slice(chunk * LANES, (chunk + 1) * LANES)
            spread[0:ANGLES, here] = high
            spread[ANGLES:2 * ANGLES, here] = low
            spread[2 * ANGLES:3 * ANGLES, here] = high
            spread[3 * ANGLES:4 * ANGLES, here] = jnp.zeros_like(high)

    cell = (lax.broadcasted_iota(jnp.int32, (block, LANES), 0) + part * block).astype(jnp.float32)
    lane = lax.broadcasted_iota(jnp.int32, (block, LANES), 1)
    weight = depth_weight(cell, row_ref[0:1, :])
    high = weight.astype(jnp.bfloat16).astype(jnp.float32)
    weight = jnp.where(lane < 2 * ANGLES, high, weight - high).astype(jnp.bfloat16)
    update = dot(weight, spread[...])
    out_ref[0] = jnp.maximum(0.0, volume_ref[0] + norm_ref[0] * update)


def exchange_kernel(
    sino, aux, wanted, measured_hbm, norm_hbm, back, residual,
    every, every_aux, measured, norm, weight, ratio, partial, from_sibling, ahead, from_far,
    linear, arrived, load_sem, send_sem, recv_sem, aux_send, aux_recv, far_send, far_recv,
    near_send, near_recv, pass_send, pass_recv, aux2_send, aux2_recv, sum_send, sum_recv,
    out_send, out_recv,
):
    g, m = lax.axis_index("grp"), lax.axis_index("blk")
    core, y_lo = g % 2, g // 2
    y_hi, z, x = m // 16, (m // 4) % 4, m % 4
    sibling = (y_lo * 2 + (1 - core), m)
    far = ((1 - y_lo) * 2 + core, m)
    far_sibling = (1 - y_lo) * 2 + (1 - core)

    def partner(d):
        flip = d // 16
        return ((y_lo + flip) % 2) * 2 + core, ((y_hi + flip) % 2) * 16 + ((z + (d // 4) % 4) % 4) * 4 + (x + d % 4) % 4

    def source(d):
        flip = d // 16
        return ((y_hi + flip) % 2) * 16 + ((z + 4 - (d // 4) % 4) % 4) * 4 + (x + 4 - d % 4) % 4

    def slot(group, member, members=1):
        return pl.ds(pl.multiple_of((group * 32 + member) * 16, 16), members * 16)

    load = [
        pltpu.make_async_copy(measured_hbm, measured, load_sem.at[0]),
        pltpu.make_async_copy(norm_hbm, norm, load_sem.at[1]),
    ]
    for copy in load:
        copy.start()

    barrier = pltpu.get_barrier_semaphore()

    def greet(d, carry):
        pl.semaphore_signal(barrier, inc=1, device_id=partner(d), device_id_type=MESH)
        return carry

    lax.fori_loop(1, 32, greet, 0)
    for device in (sibling, far):
        pl.semaphore_signal(barrier, inc=1, device_id=device, device_id_type=MESH)
    pl.semaphore_wait(barrier, 33)

    def remote(source_ref, target_ref, send, recv, device):
        return pltpu.make_async_remote_copy(
            src_ref=source_ref, dst_ref=target_ref, send_sem=send, recv_sem=recv,
            device_id=device, device_id_type=MESH,
        )

    def first_copy(d, member_from):
        device = partner(d)
        return remote(
            sino.at[slot(0, device[1])], every.at[slot(device[0] if member_from is None else g, m if member_from is None else member_from)],
            send_sem.at[d], recv_sem.at[d], device,
        )

    def first_aux(d, member_from):
        device = partner(d)
        row = device[0] * 32 + m if member_from is None else g * 32 + member_from
        return remote(aux.at[device[1]], every_aux.at[row], aux_send.at[d], aux_recv.at[d], device)

    def send(d, carry):
        first_aux(d, None).start()
        first_copy(d, None).start()
        return carry

    lax.fori_loop(1, 32, send, 0)
    every[slot(g, m)] = sino[slot(0, m)]
    every_aux[g * 32 + m] = aux[m]

    def run(group, k):
        return slot(group, ((y_hi + k // 4) % 2) * 16 + ((z + 4 - k % 4) % 4) * 4, 4)

    def to_far(k, group):
        return remote(every.at[run(group, k)], every.at[run(group, k)], far_send.at[k], far_recv.at[k], far)

    def to_near(k, group):
        return remote(every.at[run(group, k)], every.at[run(group, k)], near_send.at[k], near_recv.at[k], sibling)

    def pass_on(k, group):
        return remote(every.at[run(group, k)], every.at[run(group, k)], pass_send.at[k], pass_recv.at[k], sibling)

    def hand(k, carry):
        def arrive(d, carry):
            first_copy(d, source(d)).wait_recv()
            first_aux(d, source(d)).wait_recv()
            return carry

        lax.fori_loop(jnp.where(k == 0, 1, 4 * k), 4 * k + 4, arrive, 0)
        to_far(k, g).start()
        to_near(k, g).start()
        return carry

    lax.fori_loop(0, 8, hand, 0)

    def aux_copy(number, group, device):
        rows = pl.ds(group * 32, 32)
        return remote(every_aux.at[rows], every_aux.at[rows], aux2_send.at[number], aux2_recv.at[number], device)

    aux_copy(0, g, far).start()
    aux_copy(1, g, sibling).start()
    aux_copy(0, far[0], far).wait_recv()
    aux_copy(2, far[0], sibling).start()

    def forward_on(k, carry):
        to_far(k, far[0]).wait_recv()
        pass_on(k, far[0]).start()
        return carry

    lax.fori_loop(0, 8, forward_on, 0)
    aux_copy(1, sibling[0], sibling).wait_recv()
    aux_copy(2, far_sibling, sibling).wait_recv()

    table = every_aux[...].reshape(ANGLES * 4, LANES)
    offset = wanted[0:1, :] - table[:, 16:17]
    tall = [None] * 8
    for q in range(2):
        value = jnp.zeros_like(offset)
        for r in range(FOOT):
            value = jnp.where(offset == float(r), table[:, q * FOOT + r:q * FOOT + r + 1], value)
        for h in range(4):
            tall[h * 2 + q] = value[h * 32:(h + 1) * 32]
    tall = jnp.concatenate(tall, axis=0)
    tall_high, tall_low = halves(tall)
    for h in range(4):
        weight[h * 128:h * 128 + 64, :] = tall_high[h * 64:(h + 1) * 64]
        weight[h * 128 + 64:(h + 1) * 128, :] = tall_low[h * 64:(h + 1) * 64]
    wide_high, wide_low = halves(tall.T[:ROWS])
    wide = jnp.concatenate([wide_high, wide_high, wide_low], axis=1)

    def settle(k, carry):
        to_near(k, sibling[0]).wait_recv()
        pass_on(k, far_sibling).wait_recv()
        return carry

    lax.fori_loop(0, 8, settle, 0)
    for copy in load:
        copy.wait()

    for pair in range(4):
        columns = []
        for chunk in (2 * pair, 2 * pair + 1):
            columns.append(jnp.concatenate(
                [every[pl.ds(h * 512 + q * 8 + chunk, 32, stride=16), :] for h in range(4) for q in range(2)], axis=0
            ))
        high, low = halves(jnp.concatenate(columns, axis=1))
        forward = dot(wide, jnp.concatenate([high, low, high], axis=0))
        for side in range(2):
            chunk = 2 * pair + side
            rows = pl.ds(chunk, ROWS, stride=8)
            value = norm[rows, :] * (measured[rows, :] - forward[:, side * LANES:(side + 1) * LANES])
            residual[rows, :] = value
            ratio[:, chunk * LANES:(chunk + 1) * LANES] = value.astype(jnp.bfloat16)

    def part_of(group):
        both = dot(weight[pl.ds(pl.multiple_of(group * 128, 128), 128), :ROWS], ratio[...])
        return both[:64] + both[64:]

    def to_sibling(number):
        return remote(partial.at[number], from_sibling.at[number], sum_send.at[number], sum_recv.at[number], sibling)

    partial[0] = part_of(far_sibling)
    to_sibling(0).start()
    partial[1] = part_of(sibling[0])
    to_sibling(1).start()
    ahead[...] = part_of(far[0])
    to_sibling(0).wait_recv()
    ahead[...] += from_sibling[0]
    over = remote(ahead, from_far, sum_send.at[2], sum_recv.at[2], far)
    over.start()
    own = part_of(g)
    to_sibling(1).wait_recv()
    own = own + from_sibling[1]
    over.wait_recv()
    own = own + from_far[...]
    for q in range(2):
        for chunk in range(8):
            linear[pl.ds(q * 8 + chunk, 32, stride=16), :] = own[q * 32:(q + 1) * 32, chunk * LANES:(chunk + 1) * LANES]

    def last_copy(d, member_from):
        device = partner(d)
        return remote(
            linear.at[slot(0, device[1])], arrived.at[slot(0, m if member_from is None else member_from)],
            out_send.at[d], out_recv.at[d], device,
        )

    def give(d, carry):
        last_copy(d, None).start()
        return carry

    lax.fori_loop(1, 32, give, 0)
    arrived[slot(0, m)] = linear[slot(0, m)]

    def take(d, carry):
        last_copy(d, source(d)).wait_recv()
        return carry

    lax.fori_loop(1, 32, take, 0)
    back[...] = arrived[...]

    def sent(d, carry):
        first_copy(d, None).wait_send()
        first_aux(d, None).wait_send()
        last_copy(d, None).wait_send()
        return carry

    lax.fori_loop(1, 32, sent, 0)

    def sent_runs(k, carry):
        to_far(k, g).wait_send()
        to_near(k, g).wait_send()
        pass_on(k, far[0]).wait_send()
        return carry

    lax.fori_loop(0, 8, sent_runs, 0)
    aux_copy(0, g, far).wait_send()
    aux_copy(1, g, sibling).wait_send()
    aux_copy(2, far[0], sibling).wait_send()
    to_sibling(0).wait_send()
    to_sibling(1).wait_send()
    over.wait_send()


def shards(volume, voxel_norm, measured, ray_norm, axial_weights, row_start, row_order, subset):
    f32, bf16 = jnp.float32, jnp.bfloat16
    g, m = lax.axis_index("grp"), lax.axis_index("blk")
    sine = jnp.sin(2.0 * math.pi / TOTAL_ANG * subset.astype(f32))
    sine_wide = jnp.broadcast_to(sine[:, None], (ANGLES, LANES))
    sine_row = jnp.broadcast_to(jnp.tile(sine, 4)[None, :], (8, LANES))
    starts = lax.dynamic_slice_in_dim(row_start, g * 32 + m, 1, 1).astype(f32)
    aux = jnp.concatenate(
        [axial_weights[0], axial_weights[1], starts, jnp.zeros((ANGLES, LANES - 17), f32)], axis=1
    ).reshape(ANGLES, 1, LANES)
    wanted = lax.dynamic_slice_in_dim(row_order, g * ROWS, ROWS, 0).astype(f32)
    wanted = jnp.broadcast_to(jnp.pad(wanted, (0, 64), constant_values=-1000.0)[None, :], (8, 256))

    block = 256
    whole = lambda shape: pl.BlockSpec(shape, lambda z, y: (0,) * len(shape))
    sliced = pl.BlockSpec((1, block, COLS), lambda z, y: (z, y, 0))
    sino = pl.pallas_call(
        forward_kernel,
        grid=(2, DEPTH // block),
        in_specs=[whole((ANGLES, LANES)), sliced],
        out_specs=whole((512, LANES)),
        out_shape=jax.ShapeDtypeStruct((512, LANES), f32),
        scratch_shapes=[pltpu.VMEM((ANGLES, COLS), f32)],
        compiler_params=pltpu.CompilerParams(vmem_limit_bytes=16 << 20),
        cost_estimate=pl.CostEstimate(flops=6 * 64 * DEPTH * COLS, bytes_accessed=4 * 2 * DEPTH * COLS, transcendentals=0),
        name="forward",
    )(sine_wide, volume)

    vmem = pl.BlockSpec(memory_space=pltpu.VMEM)
    dma = pltpu.SemaphoreType.DMA
    back, residual = pl.pallas_call(
        exchange_kernel,
        in_specs=[vmem, vmem, vmem, pl.BlockSpec(memory_space=pl.ANY), pl.BlockSpec(memory_space=pl.ANY)],
        out_specs=(vmem, vmem),
        out_shape=(jax.ShapeDtypeStruct((512, LANES), f32), jax.ShapeDtypeStruct((ROWS * 8, LANES), f32)),
        scratch_shapes=[
            pltpu.VMEM((2048, LANES), f32), pltpu.VMEM((128, 1, LANES), f32),
            pltpu.VMEM((ROWS * 8, LANES), f32), pltpu.VMEM((ROWS * 8, LANES), f32),
            pltpu.VMEM((512, 256), bf16), pltpu.VMEM((ROWS, CELLS), bf16),
            pltpu.VMEM((2, 64, CELLS), f32), pltpu.VMEM((2, 64, CELLS), f32),
            pltpu.VMEM((64, CELLS), f32), pltpu.VMEM((64, CELLS), f32),
            pltpu.VMEM((512, LANES), f32), pltpu.VMEM((512, LANES), f32),
            dma((2,)), dma((32,)), dma((32,)), dma((32,)), dma((32,)), dma((8,)), dma((8,)),
            dma((8,)), dma((8,)), dma((8,)), dma((8,)), dma((3,)), dma((3,)), dma((3,)), dma((3,)),
            dma((32,)), dma((32,)),
        ],
        compiler_params=pltpu.CompilerParams(collective_id=0, has_side_effects=True, vmem_limit_bytes=24 << 20),
        cost_estimate=pl.CostEstimate(flops=2 * 6 * 192 * 256 * 1024, bytes_accessed=4 << 20, transcendentals=0),
        name="exchange",
    )(sino, aux, wanted, measured.reshape(ROWS * 8, LANES), ray_norm.reshape(ROWS * 8, LANES))

    new_volume = pl.pallas_call(
        final_kernel,
        grid=(2, DEPTH // block),
        in_specs=[whole((ANGLES, LANES)), whole((8, LANES)), whole((512, LANES)), sliced, sliced],
        out_specs=sliced,
        out_shape=jax.ShapeDtypeStruct(volume.shape, f32),
        scratch_shapes=[pltpu.VMEM((LANES, COLS), bf16)],
        compiler_params=pltpu.CompilerParams(vmem_limit_bytes=24 << 20),
        cost_estimate=pl.CostEstimate(flops=6 * 64 * DEPTH * COLS, bytes_accessed=4 * 6 * DEPTH * COLS, transcendentals=0),
        name="final",
    )(sine_wide, sine_row, back, volume, voxel_norm)
    return new_volume, residual.reshape(measured.shape)


def solution(mesh):
    placed = (
        P(("grp", "blk"), None, None),
        P(("grp", "blk"), None, None),
        P("grp", "blk", None),
        P("grp", "blk", None),
        P(("grp", "blk"), None, None),
        P(),
        P(),
        P(),
    )
    return jax.shard_map(
        shards,
        mesh=mesh,
        in_specs=placed,
        out_specs=(P(("grp", "blk"), None, None), P("grp", "blk", None)),
        check_vma=False,
    )
```

time: 560 us -> 63 us (0.11)
  the two profiles are of different devices: /device:TPU:1 before, /device:TPU:0 now
where the time goes in v1:
time: 63 us; the launch traced here: 62.6 us
  Pallas kernels  50.6 us (80%)
  local copies, waits for them, and re-layouts  8.92 us (14%)
  other arithmetic  2.34 us (4%)
  between operations  0.69 us (1%)
    pallas_call x1, Pallas kernels, shards(): pl.pallas_call(exchange_kernel, in_specs=[vmem, vmem, vmem, pl.BlockSpec(...  43 us
    unnamed x13, local copies, waits for them, and re-layouts  7.97 us
    pallas_call x1, Pallas kernels, shards(): pl.pallas_call(final_kernel, grid=(2, DEPTH // block), in_specs=[whole((A...  4.85 us
    pallas_call x1, Pallas kernels, shards(): pl.pallas_call(forward_kernel, grid=(2, DEPTH // block), in_specs=[whole(...  2.74 us

profile of v1, /device:TPU:0, one launch (start us, length us, event | category | flops | bytes accessed | tf_op | source)
XLA Modules:
  0.0 62.6 jit_solution(7303762359857954032)
XLA Ops:
  0.6 0.7 %multiply_sine_fusion = f32[32]{0:T(128)S(1)} fusion(s32[32]{0:T(128)} %param.15), kind=kLoop, calls=%fused_computation.3 | loop fusion | flops 64 | bytes 256 | tf_op jit(solution)/shard_map/sin | solution.py:359
  1.3 0.8 %dynamic-slice_convert_fusion.1 = f32[192]{0:T(256)S(1)} fusion(s32[768]{0:T(1024)} %param.14, s32[]{:T(128)S(6)} %select_n.7), kind=kLoop, calls=%fused_computation.2 | loop fusion | flops 192 | bytes 1540 | tf_op jit(solution)/shard_map/convert_element_type | solution.py:366
  2.1 0.1 pad.8.clone
  2.2 0.1 broadcast_in_dim.11
  2.3 0.7 %fusion = (f32[1,32,8]{1,2,0:T(8,128)S(1)}, f32[1,32,8]{1,2,0:T(8,128)S(1)}) fusion(f32[2,32,8]{1,2,0:T(8,128)} %param.12), kind=kLoop, calls=%fused_computation.4 | loop fusion | bytes 4096 | tf_op jit(solution)/shard_map/slice | solution.py:364
  3.0 0.1 copy.13
  3.1 0.1 broadcast_in_dim.10.sine_ref
  3.1 0.8 %dynamic-slice_convert_fusion = f32[32,1]{1,0:T(8,128)S(1)} fusion(s32[32,128]{1,0:T(8,128)} %param.13, s32[]{:T(128)S(6)} %select_n.6), kind=kLoop, calls=%fused_computation.1 | loop fusion | flops 32 | bytes 260 | tf_op jit(solution)/shard_map/convert_element_type | solution.py:362
  3.9 0.1 copy.14
  4.0 0.1 maximum_maximum_fusion
  4.1 0.0 copy-start
  4.1 2.3 %copy-done = f32[2,768,768]{2,1,0:T(8,128)S(1)} copy-done((f32[2,768,768]{2,1,0:T(8,128)S(1)}, f32[2,768,768]{2,1,0:T(8,128)}, u32[]{:S(2)}) %copy-start) | copy-done | bytes 4718616
  6.4 0.0 copy-start.1
  6.4 2.7 %forward.1.sino = f32[512,128]{1,0:T(8,128)S(1)} custom-call(f32[32,128]{1,0:T(8,128)S(1)} %broadcast_in_dim.10.sine_ref, f32[2,768,768]{2,1,0:T(8,128)S(1)} %copy-done), custom_call_target="tpu_custom_call" | custom-call | flops 226492416 | bytes 4718592 | tf_op jit(solution)/shard_map/forward/pallas_call | solution.py:372
  9.2 0.0 copy-start.3
  9.2 1.1 %copy-done.3 = f32[192,1,1024]{2,1,0:T(1,128)S(1)} copy-done((f32[192,1,1024]{2,1,0:T(1,128)S(1)}, f32[192,1,1024]{2,1,0:T(1,128)}, u32[]{:S(2)}) %copy-start.3) | copy-done | bytes 786456
  10.3 0.0 copy-start.4
  10.3 1.1 %copy-done.4 = f32[192,1,1024]{2,1,0:T(1,128)S(1)} copy-done((f32[192,1,1024]{2,1,0:T(1,128)S(1)}, f32[192,1,1024]{2,1,0:T(1,128)}, u32[]{:S(2)}) %copy-start.4) | copy-done | bytes 786456
  11.4 43.0 %exchange.1 = (f32[512,128]{1,0:T(8,128)S(1)}, f32[1536,128]{1,0:T(8,128)S(1)}) custom-call(f32[512,128]{1,0:T(8,128)S(1)} %forward.1.sino, f32[32,1,128]{2,1,0:T(1,128)S(1)} %bitcast.7, f32[8,256]{1,0:T(8,128)S(1)} %broadcast_in_dim.26.wanted, f32[1536,128]{1,0:T(8,128)S(1)} %bitcast.8, f32[1536,128]{1,0:T(8,128)S(1)} %bitcast.9), custom_call_target="tpu_custom_call" | custom-call | flops 603979776 | bytes 4194304 | tf_op jit(solution)/shard_map/exchange/pallas_call | solution.py:386
  54.5 0.0 copy-done.1
  54.5 0.0 copy-start.2
  54.5 2.3 %copy-done.2 = f32[2,768,768]{2,1,0:T(8,128)S(1)} copy-done((f32[2,768,768]{2,1,0:T(8,128)S(1)}, f32[2,768,768]{2,1,0:T(8,128)}, u32[]{:S(2)}) %copy-start.2) | copy-done | bytes 4718616
  56.8 4.9 %final.1 = f32[2,768,768]{2,1,0:T(8,128)} custom-call(f32[32,128]{1,0:T(8,128)S(1)} %broadcast_in_dim.10.sine_ref, f32[8,128]{1,0:T(8,128)S(1)} %broadcast_in_dim.24.row_ref, f32[512,128]{1,0:T(8,128)S(1)} %get-tuple-element.4.back_ref, f32[2,768,768]{2,1,0:T(8,128)S(1)} %copy-done.1, f32[2,768,768]{2,1,0:T(8,128)S(1)} %copy-done.2), custom_call_target="tpu_custom_call" | custom-call | flops 226492416 | bytes 14155776 | tf_op jit(solution)/shard_map/final/pallas_call | solution.py:407
  61.7 0.9 %copy.16 = f32[192,1,1024]{2,1,0:T(1,128)} copy(f32[192,1,1024]{2,1,0:T(1,128)S(1)} %bitcast.6) | data formatting | bytes 1572864
  (5 shorter events, 0.0 us)
Async XLA Ops:
  4.1 2.3 %copy-start = (f32[2,768,768]{2,1,0:T(8,128)S(1)}, f32[2,768,768]{2,1,0:T(8,128)}, u32[]{:S(2)}) copy-start(f32[2,768,768]{2,1,0:T(8,128)} %volume_ref.3) | copy-start | bytes 14155780
  6.4 48.1 %copy-start.1 = (f32[2,768,768]{2,1,0:T(8,128)S(1)}, f32[2,768,768]{2,1,0:T(8,128)}, u32[]{:S(2)}) copy-start(f32[2,768,768]{2,1,0:T(8,128)} %volume_ref.3) | copy-start | bytes 14155780
  9.2 1.1 %copy-start.3 = (f32[192,1,1024]{2,1,0:T(1,128)S(1)}, f32[192,1,1024]{2,1,0:T(1,128)}, u32[]{:S(2)}) copy-start(f32[192,1,1024]{2,1,0:T(1,128)} %param.10) | copy-start | bytes 2359300
  10.3 1.1 %copy-start.4 = (f32[192,1,1024]{2,1,0:T(1,128)S(1)}, f32[192,1,1024]{2,1,0:T(1,128)}, u32[]{:S(2)}) copy-start(f32[192,1,1024]{2,1,0:T(1,128)} %param.11) | copy-start | bytes 2359300
  54.5 2.3 %copy-start.2 = (f32[2,768,768]{2,1,0:T(8,128)S(1)}, f32[2,768,768]{2,1,0:T(8,128)}, u32[]{:S(2)}) copy-start(f32[2,768,768]{2,1,0:T(8,128)} %norm_ref.1) | copy-start | bytes 14155780

commit v2 on v1

v2 whole, which is shorter than its diff:
```python
import math

import jax
import jax.numpy as jnp
from jax import lax
from jax.experimental import pallas as pl
from jax.experimental.pallas import tpu as pltpu
from jax.sharding import PartitionSpec as P

TOTAL_ANG = 1024
MESH = pl.DeviceIdType.MESH
LANES = 128
ANGLES = 32
FOOT = 8
COLS = 768
DEPTH = 768
CELLS = 1024
ROWS = 192
PARTS = 3
STEP = 0.8 * CELLS / COLS


def halves(value):
    high = value.astype(jnp.bfloat16)
    return high, (value - high.astype(jnp.float32)).astype(jnp.bfloat16)


def dot(left, right):
    return jnp.dot(left, right, preferred_element_type=jnp.float32)


def depth_weight(cell, sine):
    middle = (DEPTH - 1) / 2.0 * (1.0 + 0.8 * sine)
    bump = jnp.maximum(0.0, 1.0 - jnp.abs(cell - middle) / (0.1 * DEPTH))
    return (1.0 + 2.0 * bump) / DEPTH


def centre_of(col, shift):
    return ((CELLS - 1) / 2.0 + STEP * (col - (COLS - 1) / 2.0)) + shift


def pick(tiles, first, last, index):
    inside = index & (LANES - 1)
    tile = index >> 7
    value = None
    for number in range(first, last + 1):
        found = jnp.take_along_axis(tiles[number], inside, axis=1, mode="promise_in_bounds")
        value = found if value is None else jnp.where(tile == number, found, value)
    return value


def span(low, high, tiles):
    first = max(0, min(tiles - 1, math.floor(low) // LANES))
    return first, max(first, min(tiles - 1, math.floor(high) // LANES))


def sines(subset_ref, which):
    chosen = jnp.zeros_like(which)
    for angle in range(ANGLES):
        chosen = jnp.where(which == angle, subset_ref[angle], chosen)
    return jnp.sin(2.0 * math.pi / TOTAL_ANG * chosen.astype(jnp.float32))


def ray_sums(tiles, shift, chunk):
    lane = lax.broadcasted_iota(jnp.int32, (ANGLES, LANES), 1).astype(jnp.float32)
    detector = lane + chunk * LANES
    nearest = jnp.floor((detector - (CELLS - 1) / 2.0 - shift) * (1.0 / STEP) + (COLS - 1) / 2.0)
    middle = (chunk * LANES - (CELLS - 1) / 2.0) / STEP + (COLS - 1) / 2.0
    first, last = span(middle - 49.5, middle + 49.5 + 128 / STEP + 1, COLS // LANES)
    values, total = [0.0, 0.0], 0.0
    for near in (0.0, 1.0):
        col = nearest + near
        weight = jnp.maximum(0.0, 1.0 - jnp.abs(detector - centre_of(col, shift)))
        weight = jnp.where((col >= 0.0) & (col <= COLS - 1.0), weight, 0.0)
        index = col.astype(jnp.int32)
        values = [value + weight * pick(tile, first, last, index) for value, tile in zip(values, tiles)]
        total = total + weight
    return values, total


def spread_rows(tiles, shift, chunk):
    lane = lax.broadcasted_iota(jnp.int32, (ANGLES, LANES), 1).astype(jnp.float32)
    centre = centre_of(lane + chunk * LANES, shift)
    left = jnp.floor(centre)
    middle = (CELLS - 1) / 2.0 + STEP * (chunk * LANES - (COLS - 1) / 2.0)
    first, last = span(middle - 52.5, middle + 52.5 + STEP * 128 + 1, CELLS // LANES)
    value = 0.0
    for near in (0.0, 1.0):
        detector = left + near
        weight = jnp.maximum(0.0, 1.0 - jnp.abs(detector - centre))
        value = value + weight * pick(tiles, first, last, detector.astype(jnp.int32))
    return value


def main_kernel(
    subset, row_start, order, axial, volume_hbm, scale_hbm, measured_hbm, norm_hbm,
    back, residual, volume, scale,
    measured, norm, rowsum, straight, sino, aux, every, every_aux, every_wide, weight, wide, mean,
    ratio, ahead, from_far, own, linear, arrived,
    volume_sem, load_sem, send_sem, recv_sem, aux_send, aux_recv, far_send, far_recv,
    near_send, near_recv, pass_send, pass_recv, aux2_send, aux2_recv, ratio_send, ratio_recv,
    sum_send, sum_recv, out_send, out_recv,
):
    f32, bf16 = jnp.float32, jnp.bfloat16
    block = DEPTH // PARTS
    g, m = lax.axis_index("grp"), lax.axis_index("blk")
    core, y_lo = g % 2, g // 2
    y_hi, z, x = m // 16, (m // 4) % 4, m % 4
    sibling = (y_lo * 2 + (1 - core), m)
    far = ((1 - y_lo) * 2 + core, m)
    far_sibling = (1 - y_lo) * 2 + (1 - core)

    def partner(d):
        flip = d // 16
        return ((y_lo + flip) % 2) * 2 + core, ((y_hi + flip) % 2) * 16 + ((z + (d // 4) % 4) % 4) * 4 + (x + d % 4) % 4

    def source(d):
        flip = d // 16
        return ((y_hi + flip) % 2) * 16 + ((z + 4 - (d // 4) % 4) % 4) * 4 + (x + 4 - d % 4) % 4

    def slot(group, member, members=1):
        return pl.ds(pl.multiple_of((group * 32 + member) * 16, 16), members * 16)

    def remote(source_ref, target_ref, send, recv, device):
        return pltpu.make_async_remote_copy(
            src_ref=source_ref, dst_ref=target_ref, send_sem=send, recv_sem=recv,
            device_id=device, device_id_type=MESH,
        )

    bring = []
    for q in range(2):
        for part in range(PARTS):
            here = pl.ds(part * block, block)
            bring.append(pltpu.make_async_copy(volume_hbm.at[q, here], volume.at[q, here], volume_sem.at[q * PARTS + part]))
    for copy in bring:
        copy.start()
    load = [
        pltpu.make_async_copy(measured_hbm, measured, load_sem.at[0]),
        pltpu.make_async_copy(norm_hbm, norm, load_sem.at[1]),
        pltpu.make_async_copy(scale_hbm, scale, load_sem.at[2]),
    ]
    for copy in load:
        copy.start()

    barrier = pltpu.get_barrier_semaphore()

    def greet(d, carry):
        pl.semaphore_signal(barrier, inc=1, device_id=partner(d), device_id_type=MESH)
        return carry

    lax.fori_loop(1, 32, greet, 0)
    for device in (sibling, far):
        pl.semaphore_signal(barrier, inc=1, device_id=device, device_id_type=MESH)

    sine = sines(subset, lax.broadcasted_iota(jnp.int32, (ANGLES, LANES), 0))
    shift = (0.05 * CELLS) * sine
    tiles, means = [], []
    for q in range(2):
        total = 0.0
        for part in range(PARTS):
            cell = (lax.broadcasted_iota(jnp.int32, (ANGLES, block), 1) + part * block).astype(f32)
            high, low = halves(depth_weight(cell, sine[:, :1]))
            bring[q * PARTS + part].wait()
            volume_high, volume_low = halves(volume[q, part * block:(part + 1) * block, :])
            both = dot(jnp.concatenate([high, low], axis=0), volume_high)
            total = total + (both[:ANGLES] + (both[ANGLES:] + dot(high, volume_low)))
        middle = jnp.sum(total, axis=1, keepdims=True) * (1.0 / COLS)
        means.append(middle)
        total = total - middle
        tiles.append([total[:, t * LANES:(t + 1) * LANES] for t in range(COLS // LANES)])
    for chunk in range(CELLS // LANES):
        values, sums = ray_sums(tiles, shift, chunk)
        rowsum[:, chunk * LANES:(chunk + 1) * LANES] = sums
        for q in range(2):
            straight[pl.ds(q * 8 + chunk, ANGLES, stride=16), :] = values[q]
    sino[...] = straight[...].astype(bf16)

    lane = lax.broadcasted_iota(jnp.int32, (ANGLES, LANES), 1)
    first = jnp.sum(jnp.where(lane == g * 32 + m, row_start[...], 0), axis=1, keepdims=True).astype(f32)
    table = jnp.concatenate([axial[...].reshape(16, ANGLES), jnp.zeros((16, LANES - ANGLES), f32)], axis=1)
    table = jnp.concatenate([table, jnp.zeros((LANES - 16, LANES), f32)], axis=0).T[:ANGLES]
    for number, column in ((16, first), (17, means[0]), (18, means[1])):
        table = jnp.where(lane == number, column, table)
    aux[...] = table.reshape(ANGLES, 1, LANES)

    pl.semaphore_wait(barrier, 33)

    def first_copy(d, group, member):
        device = partner(d)
        return remote(sino.at[slot(0, device[1])], every.at[slot(group, member)], send_sem.at[d], recv_sem.at[d], device)

    def first_aux(d, group, member):
        device = partner(d)
        return remote(aux.at[device[1]], every_aux.at[group * 32 + member], aux_send.at[d], aux_recv.at[d], device)

    def send_rows(d, carry):
        first_copy(d, partner(d)[0], m).start()
        return carry

    def send_aux(d, carry):
        first_aux(d, partner(d)[0], m).start()
        return carry

    lax.fori_loop(1, 32, send_rows, 0)
    lax.fori_loop(1, 32, send_aux, 0)
    every[slot(g, m)] = sino[slot(0, m)]
    every_aux[g * 32 + m] = aux[m]

    def run(group, k):
        return slot(group, ((y_hi + k // 4) % 2) * 16 + ((z + 4 - k % 4) % 4) * 4, 4)

    def to_far(k, group):
        return remote(every.at[run(group, k)], every.at[run(group, k)], far_send.at[k], far_recv.at[k], far)

    def to_near(k, group):
        return remote(every.at[run(group, k)], every.at[run(group, k)], near_send.at[k], near_recv.at[k], sibling)

    def pass_on(k, group):
        return remote(every.at[run(group, k)], every.at[run(group, k)], pass_send.at[k], pass_recv.at[k], sibling)

    def hand(k, carry):
        def arrive(d, carry):
            first_copy(d, g, source(d)).wait_recv()
            return carry

        lax.fori_loop(jnp.where(k == 0, 1, 4 * k), 4 * k + 4, arrive, 0)
        to_far(k, g).start()
        to_near(k, g).start()
        return carry

    lax.fori_loop(0, 8, hand, 0)

    def aux_copy(number, group, device):
        rows = pl.ds(group * 32, 32)
        return remote(every_aux.at[rows], every_aux.at[rows], aux2_send.at[number], aux2_recv.at[number], device)

    def arrive_aux(d, carry):
        first_aux(d, g, source(d)).wait_recv()
        return carry

    lax.fori_loop(1, 32, arrive_aux, 0)
    aux_copy(0, g, far).start()
    aux_copy(1, g, sibling).start()

    def forward_on(k, carry):
        to_far(k, far[0]).wait_recv()
        pass_on(k, far[0]).start()
        return carry

    lax.fori_loop(0, 8, forward_on, 0)
    aux_copy(0, far[0], far).wait_recv()
    aux_copy(2, far[0], sibling).start()
    aux_copy(1, sibling[0], sibling).wait_recv()
    aux_copy(2, far_sibling, sibling).wait_recv()

    table = every_aux[...].reshape(4 * ANGLES, LANES)
    rows = order[...].astype(f32)
    lower = jnp.concatenate([rows[i:i + 1] for i in range(3)], axis=1)
    upper = jnp.concatenate([rows[i:i + 1] for i in range(3, 6)], axis=1)
    offset = jnp.where(y_lo == 0, lower, upper) - table[:, 16:17]
    tall, level = [None] * 8, [None] * 8
    for q in range(2):
        value = jnp.zeros_like(offset)
        for r in range(FOOT):
            value = jnp.where(offset == float(r), table[:, q * FOOT + r:q * FOOT + r + 1], value)
        for h in range(4):
            tall[h * 2 + q] = value[h * 32:(h + 1) * 32]
            level[h * 2 + q] = table[h * 32:(h + 1) * 32, 17 + q:18 + q]
    tall, level = jnp.concatenate(tall, axis=0), jnp.concatenate(level, axis=0)
    constant = jnp.sum(tall * level, axis=0, keepdims=True)
    mean[...] = jnp.broadcast_to(constant, (LANES, 2 * ROWS)).T
    tall_high, tall_low = halves(tall)
    for h in range(4):
        weight[h * 128:h * 128 + 64, :] = tall_high[h * 64:(h + 1) * 64]
        weight[h * 128 + 64:(h + 1) * 128, :] = tall_low[h * 64:(h + 1) * 64]
    wide_high, wide_low = halves(tall.T)
    wide[0] = wide_high
    wide[1] = wide_low

    def settle(k, carry):
        to_near(k, sibling[0]).wait_recv()
        pass_on(k, far_sibling).wait_recv()
        return carry

    lax.fori_loop(0, 8, settle, 0)
    for copy in load[:2]:
        copy.wait()
    every_wide[...] = every[...].astype(f32)

    mine = pl.ds(pl.multiple_of(core * ROWS, ROWS), ROWS)
    other = pl.ds(pl.multiple_of((1 - core) * ROWS, ROWS), ROWS)
    place = jnp.concatenate([wide[0, mine, :], wide[1, mine, :]], axis=0)
    own_mean = mean[mine, :]
    own_sum = rowsum[pl.ds(m, 1), :]
    ahead_weight = weight[pl.ds(pl.multiple_of(far[0] * 128, 128), 128), :]
    own_weight = weight[pl.ds(pl.multiple_of(g * 128, 128), 128), :]

    def to_sibling(pair, rows):
        here = pl.ds(pair * 256, 256)
        return remote(ratio.at[rows, here], ratio.at[rows, here], ratio_send.at[pair], ratio_recv.at[pair], sibling)

    def over(pair):
        return remote(ahead.at[pair], from_far.at[pair], sum_send.at[pair], sum_recv.at[pair], far)

    def forward(pair):
        columns = []
        for chunk in (2 * pair, 2 * pair + 1):
            columns.append(jnp.concatenate(
                [every_wide[pl.ds(h * 512 + q * 8 + chunk, 32, stride=16), :] for h in range(4) for q in range(2)], axis=0
            ))
        both = dot(place, jnp.concatenate(columns, axis=1).astype(bf16))
        value = both[:ROWS] + both[ROWS:]
        for side in range(2):
            chunk = 2 * pair + side
            here = slice(chunk * LANES, (chunk + 1) * LANES)
            found = value[:, side * LANES:(side + 1) * LANES] + own_mean * own_sum[:, here]
            rows = pl.ds(chunk, ROWS, stride=8)
            rest = norm[rows, :] * (measured[rows, :] - found)
            residual[rows, :] = rest
            ratio[mine, here] = rest.astype(bf16)
        to_sibling(pair, mine).start()

    def part_of(weights, pair):
        both = dot(weights, ratio[:, pair * 256:(pair + 1) * 256])
        return both[:64] + both[64:]

    def send_over(pair):
        to_sibling(pair, other).wait_recv()
        ahead[pair] = part_of(ahead_weight, pair).astype(bf16)
        over(pair).start()

    forward(0)
    for pair in range(1, 4):
        forward(pair)
        send_over(pair - 1)
    send_over(3)
    for pair in range(4):
        own[:, pair * 256:(pair + 1) * 256] = part_of(own_weight, pair)
    for pair in range(4):
        over(pair).wait_recv()
        value = own[:, pair * 256:(pair + 1) * 256] + from_far[pair].astype(f32)
        for q in range(2):
            for side in range(2):
                straight[pl.ds(q * 8 + 2 * pair + side, 32, stride=16), :] = value[q * 32:(q + 1) * 32, side * LANES:(side + 1) * LANES]
    linear[...] = straight[...].astype(bf16)

    def last_copy(d, member):
        device = partner(d)
        return remote(linear.at[slot(0, device[1])], arrived.at[slot(0, member)], out_send.at[d], out_recv.at[d], device)

    def give(d, carry):
        last_copy(d, m).start()
        return carry

    lax.fori_loop(1, 32, give, 0)
    arrived[slot(0, m)] = linear[slot(0, m)]

    def sent(d, carry):
        first_copy(d, partner(d)[0], m).wait_send()
        first_aux(d, partner(d)[0], m).wait_send()
        return carry

    lax.fori_loop(1, 32, sent, 0)

    def sent_runs(k, carry):
        to_far(k, g).wait_send()
        to_near(k, g).wait_send()
        pass_on(k, far[0]).wait_send()
        return carry

    lax.fori_loop(0, 8, sent_runs, 0)
    aux_copy(0, g, far).wait_send()
    aux_copy(1, g, sibling).wait_send()
    aux_copy(2, far[0], sibling).wait_send()
    for pair in range(4):
        to_sibling(pair, mine).wait_send()
        over(pair).wait_send()
    load[2].wait()

    def take(d, carry):
        last_copy(d, source(d)).wait_recv()
        return carry

    lax.fori_loop(1, 32, take, 0)
    back[...] = arrived[...]

    def given(d, carry):
        last_copy(d, m).wait_send()
        return carry

    lax.fori_loop(1, 32, given, 0)


def final_kernel(subset, back, volume, scale, residual_in, new_volume, residual, straight, spread, staged, sems, rest_sem):
    f32 = jnp.float32
    block = DEPTH // PARTS
    keep = pltpu.make_async_copy(residual_in, residual, rest_sem)
    keep.start()
    straight[...] = back[...].astype(f32)
    shift = (0.05 * CELLS) * sines(subset, lax.broadcasted_iota(jnp.int32, (ANGLES, LANES), 0))
    sine_row = sines(subset, lax.broadcasted_iota(jnp.int32, (8, LANES), 1) % ANGLES)[:1]
    weights = []
    for part in range(PARTS):
        cell = (lax.broadcasted_iota(jnp.int32, (block, LANES), 0) + part * block).astype(f32)
        lane = lax.broadcasted_iota(jnp.int32, (block, LANES), 1)
        weight = depth_weight(cell, sine_row)
        high = weight.astype(jnp.bfloat16).astype(f32)
        weights.append(jnp.where(lane < 2 * ANGLES, high, weight - high).astype(jnp.bfloat16))
    copies = []
    for q in range(2):
        tiles = [straight[pl.ds(q * 8 + chunk, ANGLES, stride=16), :] for chunk in range(CELLS // LANES)]
        for chunk in range(COLS // LANES):
            high, low = halves(spread_rows(tiles, shift, chunk))
            here = slice(chunk * LANES, (chunk + 1) * LANES)
            spread[q, 0:ANGLES, here] = high
            spread[q, ANGLES:2 * ANGLES, here] = low
            spread[q, 2 * ANGLES:3 * ANGLES, here] = high
            spread[q, 3 * ANGLES:4 * ANGLES, here] = jnp.zeros_like(high)
        for part in range(PARTS):
            here = slice(part * block, (part + 1) * block)
            update = dot(weights[part], spread[q])
            staged[q, here, :] = jnp.maximum(0.0, volume[q, here, :] + scale[q, here, :] * update)
            rows = pl.ds(part * block, block)
            copies.append(pltpu.make_async_copy(staged.at[q, rows], new_volume.at[q, rows], sems.at[q * PARTS + part]))
            copies[-1].start()
    for copy in copies:
        copy.wait()
    keep.wait()


def shards(volume, voxel_norm, measured, ray_norm, axial_weights, row_start, row_order, subset):
    f32, bf16 = jnp.float32, jnp.bfloat16
    vmem = pl.BlockSpec(memory_space=pltpu.VMEM)
    smem = pl.BlockSpec(memory_space=pltpu.SMEM)
    hbm = pl.BlockSpec(memory_space=pltpu.HBM)
    dma = pltpu.SemaphoreType.DMA
    lines = ROWS * 8
    back, residual, volume_near, scale_near = pl.pallas_call(
        main_kernel,
        in_specs=[smem, vmem, vmem, vmem, hbm, hbm, hbm, hbm],
        out_specs=(vmem, vmem, vmem, vmem),
        out_shape=(
            jax.ShapeDtypeStruct((512, LANES), bf16), jax.ShapeDtypeStruct((lines, LANES), f32),
            jax.ShapeDtypeStruct(volume.shape, f32), jax.ShapeDtypeStruct(volume.shape, f32),
        ),
        scratch_shapes=[
            pltpu.VMEM((lines, LANES), f32), pltpu.VMEM((lines, LANES), f32),
            pltpu.VMEM((ANGLES, CELLS), f32), pltpu.VMEM((512, LANES), f32), pltpu.VMEM((512, LANES), bf16),
            pltpu.VMEM((ANGLES, 1, LANES), f32), pltpu.VMEM((2048, LANES), bf16), pltpu.VMEM((128, 1, LANES), f32),
            pltpu.VMEM((2048, LANES), f32), pltpu.VMEM((512, 2 * ROWS), bf16), pltpu.VMEM((2, 2 * ROWS, 256), bf16),
            pltpu.VMEM((2 * ROWS, LANES), f32), pltpu.VMEM((2 * ROWS, CELLS), bf16),
            pltpu.VMEM((4, 64, 256), bf16), pltpu.VMEM((4, 64, 256), bf16), pltpu.VMEM((64, CELLS), f32),
            pltpu.VMEM((512, LANES), bf16), pltpu.VMEM((512, LANES), bf16),
            dma((2 * PARTS,)), dma((3,)), dma((32,)), dma((32,)), dma((32,)), dma((32,)), dma((8,)), dma((8,)),
            dma((8,)), dma((8,)), dma((8,)), dma((8,)), dma((3,)), dma((3,)), dma((4,)), dma((4,)),
            dma((4,)), dma((4,)), dma((32,)), dma((32,)),
        ],
        compiler_params=pltpu.CompilerParams(collective_id=0, has_side_effects=True, vmem_limit_bytes=28 << 20),
        cost_estimate=pl.CostEstimate(flops=10 ** 9, bytes_accessed=100 << 20, transcendentals=0),
        name="exchange",
    )(
        subset, row_start, row_order.reshape(6, LANES), jnp.transpose(axial_weights, (0, 2, 1)), volume, voxel_norm,
        measured.reshape(lines, LANES), ray_norm.reshape(lines, LANES),
    )
    new_volume, residual = pl.pallas_call(
        final_kernel,
        in_specs=[smem, vmem, vmem, vmem, pl.BlockSpec(memory_space=pl.ANY)],
        out_specs=(hbm, hbm),
        out_shape=(jax.ShapeDtypeStruct(volume.shape, f32), jax.ShapeDtypeStruct((lines, LANES), f32)),
        scratch_shapes=[
            pltpu.VMEM((512, LANES), f32), pltpu.VMEM((2, LANES, COLS), bf16), pltpu.VMEM(volume.shape, f32),
            dma((2 * PARTS,)), dma,
        ],
        compiler_params=pltpu.CompilerParams(vmem_limit_bytes=28 << 20),
        cost_estimate=pl.CostEstimate(flops=6 * 64 * DEPTH * COLS, bytes_accessed=4 * 6 * DEPTH * COLS, transcendentals=0),
        name="final",
    )(subset, back, volume_near, scale_near, residual)
    return new_volume, residual.reshape(measured.shape)


def solution(mesh):
    placed = (
        P(("grp", "blk"), None, None),
        P(("grp", "blk"), None, None),
        P("grp", "blk", None),
        P("grp", "blk", None),
        P(("grp", "blk"), None, None),
        P(),
        P(),
        P(),
    )
    return jax.shard_map(
        shards,
        mesh=mesh,
        in_specs=placed,
        out_specs=(P(("grp", "blk"), None, None), P("grp", "blk", None)),
        check_vma=False,
    )
```

time: 63 us -> 55.3 us (0.88)
  the two profiles are of different devices: /device:TPU:0 before, /device:TPU:1 now
where the time goes in v2:
time: 55.3 us; the launch traced here: 54.9 us
  Pallas kernels  44.6 us (81%)
  local copies, waits for them, and re-layouts  9.69 us (18%)
  between operations  0.66 us (1%)
    pallas_call x1, Pallas kernels, shards(): pl.pallas_call(main_kernel, in_specs=[smem, vmem, vmem, vmem, hbm, hbm, h...  40.6 us
    unnamed x16, local copies, waits for them, and re-layouts  9.69 us
    pallas_call x1, Pallas kernels, shards(): pl.pallas_call(final_kernel, in_specs=[smem, vmem, vmem, vmem, pl.BlockSp...  3.93 us

profile of v2, /device:TPU:1, one launch (start us, length us, event | category | flops | bytes accessed | tf_op | source)
XLA Modules:
  0.0 54.9 jit_solution(1785898107341038855)
XLA Ops:
  0.6 0.0 copy-start
  0.6 2.3 %copy-done = f32[2,768,768]{2,1,0:T(8,128)S(1)} copy-done((f32[2,768,768]{2,1,0:T(8,128)S(1)}, f32[2,768,768]{2,1,0:T(8,128)}, u32[]{:S(2)}) %copy-start) | copy-done | bytes 4718616
  3.0 0.0 copy-start.1
  3.0 2.3 %copy-done.1 = f32[2,768,768]{2,1,0:T(8,128)S(1)} copy-done((f32[2,768,768]{2,1,0:T(8,128)S(1)}, f32[2,768,768]{2,1,0:T(8,128)}, u32[]{:S(2)}) %copy-start.1) | copy-done | bytes 4718616
  5.3 0.0 copy-start.2
  5.3 1.1 %copy-done.2 = f32[192,1,1024]{2,1,0:T(1,128)S(1)} copy-done((f32[192,1,1024]{2,1,0:T(1,128)S(1)}, f32[192,1,1024]{2,1,0:T(1,128)}, u32[]{:S(2)}) %copy-start.2) | copy-done | bytes 786456
  6.4 0.0 copy-start.3
  6.4 1.1 %copy-done.3 = f32[192,1,1024]{2,1,0:T(1,128)S(1)} copy-done((f32[192,1,1024]{2,1,0:T(1,128)S(1)}, f32[192,1,1024]{2,1,0:T(1,128)}, u32[]{:S(2)}) %copy-start.3) | copy-done | bytes 786456
  7.6 0.0 copy-start.4
  7.6 0.7 %copy-done.4 = s32[32,128]{1,0:T(8,128)S(1)} copy-done((s32[32,128]{1,0:T(8,128)S(1)}, s32[32,128]{1,0:T(8,128)}, u32[]{:S(2)}) %copy-start.4) | copy-done | bytes 16408
  8.3 0.0 copy-start.5
  8.3 0.7 %copy-done.5 = f32[2,32,8]{1,2,0:T(8,128)S(1)} copy-done((f32[2,32,8]{1,2,0:T(8,128)S(1)}, f32[2,32,8]{1,2,0:T(8,128)}, u32[]{:S(2)}) %copy-start.5) | copy-done | bytes 2072
  9.0 0.0 copy-start.6
  9.0 0.7 %copy-done.6 = s32[768]{0:T(1024)S(1)} copy-done((s32[768]{0:T(1024)S(1)}, s32[768]{0:T(1024)}, u32[]{:S(2)}) %copy-start.6) | copy-done | bytes 3096
  9.7 0.0 copy-start.7
  9.7 0.7 %copy-done.7 = s32[32]{0:T(128)S(1)} copy-done((s32[32]{0:T(128)S(1)}, s32[32]{0:T(128)}, u32[]{:S(2)}) %copy-start.7) | copy-done | bytes 152
  10.3 40.6 %exchange.1 = (bf16[512,128]{1,0:T(8,128)(2,1)S(1)}, f32[1536,128]{1,0:T(8,128)S(1)}, f32[2,768,768]{2,1,0:T(8,128)S(1)}, f32[2,768,768]{2,1,0:T(8,128)S(1)}) custom-call(s32[32]{0:T(128)S(1)} %copy-done.7, s32[32,128]{1,0:T(8,128)S(1)} %copy-done.4, s32[6,128]{1,0:T(8,128)S(1)} %bitcast.8, f32[2,8,32]{2,1,0:T(8,128)S(1)} %bitcast.7, ...), custom_call_target="tpu_custom_call" | custom-call | flops 1000000000 | bytes 104857600 | tf_op jit(solution)/shard_map/exchange/pallas_call | solution.py:438
  51.0 3.9 %final.1 = (f32[2,768,768]{2,1,0:T(8,128)}, f32[1536,128]{1,0:T(8,128)}) custom-call(s32[32]{0:T(128)S(1)} %copy-done.7, bf16[512,128]{1,0:T(8,128)(2,1)S(1)} %get-tuple-element.8.back, f32[2,768,768]{2,1,0:T(8,128)S(1)} %get-tuple-element.9.volume, f32[2,768,768]{2,1,0:T(8,128)S(1)} %get-tuple-element.10.scale, f32[1536,128]{1,0:T(8,128)S(1)} %get-tuple-element.11.residual_in), custom_call_target="tpu_custom_call" | custom-call | flops 226492416 | bytes 14155776 | tf_op jit(solution)/shard_map/final/pallas_call | solution.py:465
Async XLA Ops:
  0.6 2.3 %copy-start = (f32[2,768,768]{2,1,0:T(8,128)S(1)}, f32[2,768,768]{2,1,0:T(8,128)}, u32[]{:S(2)}) copy-start(f32[2,768,768]{2,1,0:T(8,128)} %volume_hbm.1) | copy-start | bytes 14155780
  3.0 2.3 %copy-start.1 = (f32[2,768,768]{2,1,0:T(8,128)S(1)}, f32[2,768,768]{2,1,0:T(8,128)}, u32[]{:S(2)}) copy-start(f32[2,768,768]{2,1,0:T(8,128)} %scale_hbm.1) | copy-start | bytes 14155780
  5.3 1.1 %copy-start.2 = (f32[192,1,1024]{2,1,0:T(1,128)S(1)}, f32[192,1,1024]{2,1,0:T(1,128)}, u32[]{:S(2)}) copy-start(f32[192,1,1024]{2,1,0:T(1,128)} %param.10) | copy-start | bytes 2359300
  6.4 1.1 %copy-start.3 = (f32[192,1,1024]{2,1,0:T(1,128)S(1)}, f32[192,1,1024]{2,1,0:T(1,128)}, u32[]{:S(2)}) copy-start(f32[192,1,1024]{2,1,0:T(1,128)} %param.11) | copy-start | bytes 2359300
  7.6 0.7 %copy-start.4 = (s32[32,128]{1,0:T(8,128)S(1)}, s32[32,128]{1,0:T(8,128)}, u32[]{:S(2)}) copy-start(s32[32,128]{1,0:T(8,128)} %row_start.1) | copy-start | bytes 49156
  8.3 0.7 %copy-start.5 = (f32[2,32,8]{1,2,0:T(8,128)S(1)}, f32[2,32,8]{1,2,0:T(8,128)}, u32[]{:S(2)}) copy-start(f32[2,32,8]{1,2,0:T(8,128)} %param.12) | copy-start | bytes 6148
  9.0 0.7 %copy-start.6 = (s32[768]{0:T(1024)S(1)}, s32[768]{0:T(1024)}, u32[]{:S(2)}) copy-start(s32[768]{0:T(1024)} %param.14) | copy-start | bytes 9220
  9.7 0.7 %copy-start.7 = (s32[32]{0:T(128)S(1)}, s32[32]{0:T(128)}, u32[]{:S(2)}) copy-start(s32[32]{0:T(128)} %subset.3) | copy-start | bytes 388

commit v3 on v2

--- a/solution.py
+++ b/solution.py
@@ -93,11 +93,11 @@
 
 
 def main_kernel(
-    subset, row_start, order, axial, volume_hbm, scale_hbm, measured_hbm, norm_hbm,
-    back, residual, volume, scale,
-    measured, norm, rowsum, straight, sino, aux, every, every_aux, every_wide, weight, wide, mean,
+    subset_hbm, row_start_hbm, order_hbm, axial_hbm, volume_hbm, scale_hbm, measured_hbm, norm_hbm,
+    back, residual, volume, scale, moved, depth,
+    subset, row_start, order, axial, measured, norm, rowsum, straight, sino, aux, every, every_aux, every_wide, weight, wide, mean,
     ratio, ahead, from_far, own, linear, arrived,
-    volume_sem, load_sem, send_sem, recv_sem, aux_send, aux_recv, far_send, far_recv,
+    volume_sem, small_sem, load_sem, send_sem, recv_sem, aux_send, aux_recv, far_send, far_recv,
     near_send, near_recv, pass_send, pass_recv, aux2_send, aux2_recv, ratio_send, ratio_recv,
     sum_send, sum_recv, out_send, out_recv,
 ):
@@ -127,6 +127,14 @@
             device_id=device, device_id_type=MESH,
         )
 
+    small = [
+        pltpu.make_async_copy(subset_hbm, subset, small_sem.at[0]),
+        pltpu.make_async_copy(row_start_hbm, row_start, small_sem.at[1]),
+        pltpu.make_async_copy(axial_hbm, axial, small_sem.at[2]),
+        pltpu.make_async_copy(order_hbm, order, small_sem.at[3]),
+    ]
+    for copy in small:
+        copy.start()
     bring = []
     for q in range(2):
         for part in range(PARTS):
@@ -152,8 +160,11 @@
     for device in (sibling, far):
         pl.semaphore_signal(barrier, inc=1, device_id=device, device_id_type=MESH)
 
+    for copy in small:
+        copy.wait()
     sine = sines(subset, lax.broadcasted_iota(jnp.int32, (ANGLES, LANES), 0))
     shift = (0.05 * CELLS) * sine
+    moved[...] = shift
     tiles, means = [], []
     for q in range(2):
         total = 0.0
@@ -355,6 +366,14 @@
     lax.fori_loop(1, 32, give, 0)
     arrived[slot(0, m)] = linear[slot(0, m)]
 
+    sine_row = sines(subset, lax.broadcasted_iota(jnp.int32, (8, LANES), 1) % ANGLES)[:1]
+    for part in range(PARTS):
+        cell = (lax.broadcasted_iota(jnp.int32, (block, LANES), 0) + part * block).astype(f32)
+        lane = lax.broadcasted_iota(jnp.int32, (block, LANES), 1)
+        value = depth_weight(cell, sine_row)
+        high = value.astype(bf16).astype(f32)
+        depth[part * block:(part + 1) * block, :] = jnp.where(lane < 2 * ANGLES, high, value - high).astype(bf16)
+
     def sent(d, carry):
         first_copy(d, partner(d)[0], m).wait_send()
         first_aux(d, partner(d)[0], m).wait_send()
@@ -391,21 +410,13 @@
     lax.fori_loop(1, 32, given, 0)
 
 
-def final_kernel(subset, back, volume, scale, residual_in, new_volume, residual, straight, spread, staged, sems, rest_sem):
+def final_kernel(moved, depth, back, volume, scale, residual_in, new_volume, residual, straight, spread, staged, sems, rest_sem):
     f32 = jnp.float32
     block = DEPTH // PARTS
     keep = pltpu.make_async_copy(residual_in, residual, rest_sem)
     keep.start()
     straight[...] = back[...].astype(f32)
-    shift = (0.05 * CELLS) * sines(subset, lax.broadcasted_iota(jnp.int32, (ANGLES, LANES), 0))
-    sine_row = sines(subset, lax.broadcasted_iota(jnp.int32, (8, LANES), 1) % ANGLES)[:1]
-    weights = []
-    for part in range(PARTS):
-        cell = (lax.broadcasted_iota(jnp.int32, (block, LANES), 0) + part * block).astype(f32)
-        lane = lax.broadcasted_iota(jnp.int32, (block, LANES), 1)
-        weight = depth_weight(cell, sine_row)
-        high = weight.astype(jnp.bfloat16).astype(f32)
-        weights.append(jnp.where(lane < 2 * ANGLES, high, weight - high).astype(jnp.bfloat16))
+    shift = moved[...]
     copies = []
     for q in range(2):
         tiles = [straight[pl.ds(q * 8 + chunk, ANGLES, stride=16), :] for chunk in range(CELLS // LANES)]
@@ -418,7 +429,7 @@
             spread[q, 3 * ANGLES:4 * ANGLES, here] = jnp.zeros_like(high)
         for part in range(PARTS):
             here = slice(part * block, (part + 1) * block)
-            update = dot(weights[part], spread[q])
+            update = dot(depth[here, :], spread[q])
             staged[q, here, :] = jnp.maximum(0.0, volume[q, here, :] + scale[q, here, :] * update)
             rows = pl.ds(part * block, block)
             copies.append(pltpu.make_async_copy(staged.at[q, rows], new_volume.at[q, rows], sems.at[q * PARTS + part]))
@@ -431,19 +442,21 @@
 def shards(volume, voxel_norm, measured, ray_norm, axial_weights, row_start, row_order, subset):
     f32, bf16 = jnp.float32, jnp.bfloat16
     vmem = pl.BlockSpec(memory_space=pltpu.VMEM)
-    smem = pl.BlockSpec(memory_space=pltpu.SMEM)
     hbm = pl.BlockSpec(memory_space=pltpu.HBM)
     dma = pltpu.SemaphoreType.DMA
     lines = ROWS * 8
-    back, residual, volume_near, scale_near = pl.pallas_call(
+    back, residual, volume_near, scale_near, moved, depth = pl.pallas_call(
         main_kernel,
-        in_specs=[smem, vmem, vmem, vmem, hbm, hbm, hbm, hbm],
-        out_specs=(vmem, vmem, vmem, vmem),
+        in_specs=[hbm] * 8,
+        out_specs=(vmem,) * 6,
         out_shape=(
             jax.ShapeDtypeStruct((512, LANES), bf16), jax.ShapeDtypeStruct((lines, LANES), f32),
             jax.ShapeDtypeStruct(volume.shape, f32), jax.ShapeDtypeStruct(volume.shape, f32),
+            jax.ShapeDtypeStruct((ANGLES, LANES), f32), jax.ShapeDtypeStruct((DEPTH, LANES), bf16),
         ),
         scratch_shapes=[
+            pltpu.SMEM((ANGLES,), jnp.int32), pltpu.VMEM((ANGLES, 4 * ANGLES), jnp.int32),
+            pltpu.VMEM((6, LANES), jnp.int32), pltpu.VMEM((2, FOOT, ANGLES), f32),
             pltpu.VMEM((lines, LANES), f32), pltpu.VMEM((lines, LANES), f32),
             pltpu.VMEM((ANGLES, CELLS), f32), pltpu.VMEM((512, LANES), f32), pltpu.VMEM((512, LANES), bf16),
             pltpu.VMEM((ANGLES, 1, LANES), f32), pltpu.VMEM((2048, LANES), bf16), pltpu.VMEM((128, 1, LANES), f32),
@@ -451,7 +464,7 @@
             pltpu.VMEM((2 * ROWS, LANES), f32), pltpu.VMEM((2 * ROWS, CELLS), bf16),
             pltpu.VMEM((4, 64, 256), bf16), pltpu.VMEM((4, 64, 256), bf16), pltpu.VMEM((64, CELLS), f32),
             pltpu.VMEM((512, LANES), bf16), pltpu.VMEM((512, LANES), bf16),
-            dma((2 * PARTS,)), dma((3,)), dma((32,)), dma((32,)), dma((32,)), dma((32,)), dma((8,)), dma((8,)),
+            dma((2 * PARTS,)), dma((4,)), dma((3,)), dma((32,)), dma((32,)), dma((32,)), dma((32,)), dma((8,)), dma((8,)),
             dma((8,)), dma((8,)), dma((8,)), dma((8,)), dma((3,)), dma((3,)), dma((4,)), dma((4,)),
             dma((4,)), dma((4,)), dma((32,)), dma((32,)),
         ],
@@ -459,12 +472,14 @@
         cost_estimate=pl.CostEstimate(flops=10 ** 9, bytes_accessed=100 << 20, transcendentals=0),
         name="exchange",
     )(
-        subset, row_start, row_order.reshape(6, LANES), jnp.transpose(axial_weights, (0, 2, 1)), volume, voxel_norm,
-        measured.reshape(lines, LANES), ray_norm.reshape(lines, LANES),
+        *[pltpu.with_memory_space_constraint(array, pltpu.HBM) for array in (
+            subset, row_start, row_order.reshape(6, LANES), jnp.transpose(axial_weights, (0, 2, 1)), volume, voxel_norm,
+            measured.reshape(lines, LANES), ray_norm.reshape(lines, LANES),
+        )]
     )
     new_volume, residual = pl.pallas_call(
         final_kernel,
-        in_specs=[smem, vmem, vmem, vmem, pl.BlockSpec(memory_space=pl.ANY)],
+        in_specs=[vmem, vmem, vmem, vmem, vmem, pl.BlockSpec(memory_space=pl.ANY)],
         out_specs=(hbm, hbm),
         out_shape=(jax.ShapeDtypeStruct(volume.shape, f32), jax.ShapeDtypeStruct((lines, LANES), f32)),
         scratch_shapes=[
@@ -474,7 +489,7 @@
         compiler_params=pltpu.CompilerParams(vmem_limit_bytes=28 << 20),
         cost_estimate=pl.CostEstimate(flops=6 * 64 * DEPTH * COLS, bytes_accessed=4 * 6 * DEPTH * COLS, transcendentals=0),
         name="final",
-    )(subset, back, volume_near, scale_near, residual)
+    )(moved, depth, back, volume_near, scale_near, residual)
     return new_volume, residual.reshape(measured.shape)
 
 

time: 55.3 us -> 43.4 us (0.78)
  local copies, waits for them, and re-layouts: 9.69 us -> 0 us
  Pallas kernels: 44.6 us -> 42.6 us
    unnamed x16 -> x0, local copies, waits for them, and re-layouts: 9.69 us -> none
    pallas_call x2, Pallas kernels: 44.6 us -> 42.6 us  [the longest x1 39.4 us: shards(): pl.pallas_call(main_kernel, in_specs=[hbm] * 8, out_specs=(vmem,) * 6, ou...]
where the time goes in v3:
time: 43.4 us; the launch traced here: 43.2 us
  Pallas kernels  42.6 us (98%)
  between operations  0.64 us (1%)
    pallas_call x1, Pallas kernels, shards(): pl.pallas_call(main_kernel, in_specs=[hbm] * 8, out_specs=(vmem,) * 6, ou...  39.4 us
    pallas_call x1, Pallas kernels, shards(): pl.pallas_call(final_kernel, in_specs=[vmem, vmem, vmem, vmem, vmem, pl.B...  3.22 us

profile of v3, /device:TPU:1, one launch (start us, length us, event | category | flops | bytes accessed | tf_op | source)
XLA Modules:
  0.0 43.2 jit_solution(12009831744654962310)
XLA Ops:
  0.6 39.4 %exchange.1 = (bf16[512,128]{1,0:T(8,128)(2,1)S(1)}, f32[1536,128]{1,0:T(8,128)S(1)}, f32[2,768,768]{2,1,0:T(8,128)S(1)}, f32[2,768,768]{2,1,0:T(8,128)S(1)}, f3...) custom-call(s32[32]{0:T(128)} %subset_hbm.1, s32[32,128]{1,0:T(8,128)} %row_start_hbm.1, s32[6,128]{1,0:T(8,128)} %bitcast.8, ...), custom_call_target="tpu_custom_call" | custom-call | flops 1000000000 | bytes 104857600 | tf_op jit(solution)/shard_map/exchange/pallas_call | solution.py:448
  40.0 3.2 %final.1 = (f32[2,768,768]{2,1,0:T(8,128)}, f32[1536,128]{1,0:T(8,128)}) custom-call(f32[32,128]{1,0:T(8,128)S(1)} %get-tuple-element.10.moved, bf16[768,128]{1,0:T(8,128)(2,1)S(1)} %get-tuple-element.11.depth, bf16[512,128]{1,0:T(8,128)(2,1)S(1)} %get-tuple-element.12.back, f32[2,768,768]{2,1,0:T(8,128)S(1)} %get-tuple-element.13.volume, ...), custom_call_target="tpu_custom_call" | custom-call | flops 226492416 | bytes 14155776 | tf_op jit(solution)/shard_map/final/pallas_call | solution.py:480

commit v4 on v3

--- a/solution.py
+++ b/solution.py
@@ -96,30 +96,36 @@
     subset_hbm, row_start_hbm, order_hbm, axial_hbm, volume_hbm, scale_hbm, measured_hbm, norm_hbm,
     back, residual, volume, scale, moved, depth,
     subset, row_start, order, axial, measured, norm, rowsum, straight, sino, aux, every, every_aux, every_wide, weight, wide, mean,
-    ratio, ahead, from_far, own, linear, arrived,
-    volume_sem, small_sem, load_sem, send_sem, recv_sem, aux_send, aux_recv, far_send, far_recv,
-    near_send, near_recv, pass_send, pass_recv, aux2_send, aux2_recv, ratio_send, ratio_recv,
-    sum_send, sum_recv, out_send, out_recv,
+    ratio, linear, arrived,
+    volume_sem, small_sem, load_sem, send_sem, recv_sem, aux_send, aux_recv,
+    near_send, near_recv, aux2_send, aux2_recv, ratio_send, ratio_recv, out_send, out_recv,
 ):
     f32, bf16 = jnp.float32, jnp.bfloat16
     block = DEPTH // PARTS
     g, m = lax.axis_index("grp"), lax.axis_index("blk")
-    core, y_lo = g % 2, g // 2
-    y_hi, z, x = m // 16, (m // 4) % 4, m % 4
-    sibling = (y_lo * 2 + (1 - core), m)
-    far = ((1 - y_lo) * 2 + core, m)
-    far_sibling = (1 - y_lo) * 2 + (1 - core)
-
-    def partner(d):
-        flip = d // 16
-        return ((y_lo + flip) % 2) * 2 + core, ((y_hi + flip) % 2) * 16 + ((z + (d // 4) % 4) % 4) * 4 + (x + d % 4) % 4
-
-    def source(d):
-        flip = d // 16
-        return ((y_hi + flip) % 2) * 16 + ((z + 4 - (d // 4) % 4) % 4) * 4 + (x + 4 - d % 4) % 4
-
-    def slot(group, member, members=1):
-        return pl.ds(pl.multiple_of((group * 32 + member) * 16, 16), members * 16)
+    core = g % 2
+    y, z, x = (m // 16) * 2 + g // 2, (m // 4) % 4, m % 4
+    sibling = (g - core + (1 - core), m)
+
+    def chip(y, z, x):
+        return (y % 2) * 2 + core, (y // 2) * 16 + z * 4 + x
+
+    def spread_out(i):
+        far_first = lambda j: jnp.where(j == 0, 2, jnp.where(j == 1, 1, jnp.where(j == 2, 3, 0)))
+        return far_first(i // 16), far_first((i // 4) % 4), far_first(i % 4)
+
+    def partner(i):
+        dy, dz, dx = spread_out(i)
+        return chip((y + dy) % 4, (z + dz) % 4, (x + dx) % 4)
+
+    def source(i):
+        dy, dz, dx = spread_out(i)
+        return ((y + 4 - dy) % 4) * 16 + ((z + 4 - dz) % 4) * 4 + (x + 4 - dx) % 4
+
+    here_chip = y * 16 + z * 4 + x
+
+    def slot(number, members=1):
+        return pl.ds(pl.multiple_of(number * 16, 16), members * 16)
 
     def remote(source_ref, target_ref, send, recv, device):
         return pltpu.make_async_remote_copy(
@@ -147,18 +153,14 @@
         pltpu.make_async_copy(norm_hbm, norm, load_sem.at[1]),
         pltpu.make_async_copy(scale_hbm, scale, load_sem.at[2]),
     ]
-    for copy in load:
-        copy.start()
-
     barrier = pltpu.get_barrier_semaphore()
 
     def greet(d, carry):
         pl.semaphore_signal(barrier, inc=1, device_id=partner(d), device_id_type=MESH)
         return carry
 
-    lax.fori_loop(1, 32, greet, 0)
-    for device in (sibling, far):
-        pl.semaphore_signal(barrier, inc=1, device_id=device, device_id_type=MESH)
+    lax.fori_loop(0, 63, greet, 0)
+    pl.semaphore_signal(barrier, inc=1, device_id=sibling, device_id_type=MESH)
 
     for copy in small:
         copy.wait()
@@ -179,12 +181,14 @@
         means.append(middle)
         total = total - middle
         tiles.append([total[:, t * LANES:(t + 1) * LANES] for t in range(COLS // LANES)])
+    for copy in load:
+        copy.start()
     for chunk in range(CELLS // LANES):
         values, sums = ray_sums(tiles, shift, chunk)
         rowsum[:, chunk * LANES:(chunk + 1) * LANES] = sums
         for q in range(2):
             straight[pl.ds(q * 8 + chunk, ANGLES, stride=16), :] = values[q]
-    sino[...] = straight[...].astype(bf16)
+    sino[...] = straight[:512].astype(bf16)
 
     lane = lax.broadcasted_iota(jnp.int32, (ANGLES, LANES), 1)
     first = jnp.sum(jnp.where(lane == g * 32 + m, row_start[...], 0), axis=1, keepdims=True).astype(f32)
@@ -194,106 +198,74 @@
         table = jnp.where(lane == number, column, table)
     aux[...] = table.reshape(ANGLES, 1, LANES)
 
-    pl.semaphore_wait(barrier, 33)
-
-    def first_copy(d, group, member):
-        device = partner(d)
-        return remote(sino.at[slot(0, device[1])], every.at[slot(group, member)], send_sem.at[d], recv_sem.at[d], device)
-
-    def first_aux(d, group, member):
-        device = partner(d)
-        return remote(aux.at[device[1]], every_aux.at[group * 32 + member], aux_send.at[d], aux_recv.at[d], device)
-
-    def send_rows(d, carry):
-        first_copy(d, partner(d)[0], m).start()
-        return carry
-
-    def send_aux(d, carry):
-        first_aux(d, partner(d)[0], m).start()
-        return carry
-
-    lax.fori_loop(1, 32, send_rows, 0)
-    lax.fori_loop(1, 32, send_aux, 0)
-    every[slot(g, m)] = sino[slot(0, m)]
-    every_aux[g * 32 + m] = aux[m]
-
-    def run(group, k):
-        return slot(group, ((y_hi + k // 4) % 2) * 16 + ((z + 4 - k % 4) % 4) * 4, 4)
-
-    def to_far(k, group):
-        return remote(every.at[run(group, k)], every.at[run(group, k)], far_send.at[k], far_recv.at[k], far)
-
-    def to_near(k, group):
-        return remote(every.at[run(group, k)], every.at[run(group, k)], near_send.at[k], near_recv.at[k], sibling)
-
-    def pass_on(k, group):
-        return remote(every.at[run(group, k)], every.at[run(group, k)], pass_send.at[k], pass_recv.at[k], sibling)
-
-    def hand(k, carry):
-        def arrive(d, carry):
-            first_copy(d, g, source(d)).wait_recv()
-            return carry
-
-        lax.fori_loop(jnp.where(k == 0, 1, 4 * k), 4 * k + 4, arrive, 0)
-        to_far(k, g).start()
-        to_near(k, g).start()
-        return carry
-
-    lax.fori_loop(0, 8, hand, 0)
-
-    def aux_copy(number, group, device):
-        rows = pl.ds(group * 32, 32)
-        return remote(every_aux.at[rows], every_aux.at[rows], aux2_send.at[number], aux2_recv.at[number], device)
-
-    def arrive_aux(d, carry):
-        first_aux(d, g, source(d)).wait_recv()
-        return carry
-
-    lax.fori_loop(1, 32, arrive_aux, 0)
-    aux_copy(0, g, far).start()
-    aux_copy(1, g, sibling).start()
-
-    def forward_on(k, carry):
-        to_far(k, far[0]).wait_recv()
-        pass_on(k, far[0]).start()
-        return carry
-
-    lax.fori_loop(0, 8, forward_on, 0)
-    aux_copy(0, far[0], far).wait_recv()
-    aux_copy(2, far[0], sibling).start()
-    aux_copy(1, sibling[0], sibling).wait_recv()
-    aux_copy(2, far_sibling, sibling).wait_recv()
+    pl.semaphore_wait(barrier, 64)
+
+    def first_copy(i, number):
+        device = partner(i)
+        return remote(sino.at[slot(device[1])], every.at[slot(core * 64 + number)], send_sem.at[i], recv_sem.at[i], device)
+
+    def first_aux(i, number):
+        device = partner(i)
+        return remote(aux.at[device[1]], every_aux.at[core * 64 + number], aux_send.at[i], aux_recv.at[i], device)
+
+    def send(i, carry):
+        first_aux(i, here_chip).start()
+        first_copy(i, here_chip).start()
+        return carry
+
+    lax.fori_loop(0, 63, send, 0)
+    every[slot(core * 64 + here_chip)] = sino[slot(m)]
+    every_aux[core * 64 + here_chip] = aux[m]
+
+    def near_rows(number, side):
+        rows = slot(side * 64 + ((y + 4 - number) % 4) * 16, 16)
+        return remote(every.at[rows], every.at[rows], near_send.at[number], near_recv.at[number], sibling)
+
+    def near_aux(side):
+        rows = pl.ds(side * 64, 64)
+        return remote(every_aux.at[rows], every_aux.at[rows], aux2_send.at[0], aux2_recv.at[0], sibling)
+
+    def arrive_aux(i, carry):
+        first_aux(i, source(i)).wait_recv()
+        return carry
+
+    def arrive(i, carry):
+        first_copy(i, source(i)).wait_recv()
+        return carry
+
+    lax.fori_loop(0, 63, arrive_aux, 0)
+    near_aux(core).start()
+    for number, order_of in ((0, 3), (1, 1), (3, 2), (2, 0)):
+        lax.fori_loop(order_of * 16, order_of * 16 + (15 if number == 0 else 16), arrive, 0)
+        near_rows(number, core).start()
+    near_aux(1 - core).wait_recv()
 
     table = every_aux[...].reshape(4 * ANGLES, LANES)
     rows = order[...].astype(f32)
     lower = jnp.concatenate([rows[i:i + 1] for i in range(3)], axis=1)
     upper = jnp.concatenate([rows[i:i + 1] for i in range(3, 6)], axis=1)
-    offset = jnp.where(y_lo == 0, lower, upper) - table[:, 16:17]
-    tall, level = [None] * 8, [None] * 8
+    offset = jnp.where(y % 2 == 0, lower, upper) - table[:, 16:17]
+    tall, level = [None] * 4, [None] * 4
     for q in range(2):
         value = jnp.zeros_like(offset)
         for r in range(FOOT):
             value = jnp.where(offset == float(r), table[:, q * FOOT + r:q * FOOT + r + 1], value)
-        for h in range(4):
-            tall[h * 2 + q] = value[h * 32:(h + 1) * 32]
-            level[h * 2 + q] = table[h * 32:(h + 1) * 32, 17 + q:18 + q]
+        for side in range(2):
+            tall[side * 2 + q] = value[side * 64:(side + 1) * 64]
+            level[side * 2 + q] = table[side * 64:(side + 1) * 64, 17 + q:18 + q]
     tall, level = jnp.concatenate(tall, axis=0), jnp.concatenate(level, axis=0)
     constant = jnp.sum(tall * level, axis=0, keepdims=True)
     mean[...] = jnp.broadcast_to(constant, (LANES, 2 * ROWS)).T
     tall_high, tall_low = halves(tall)
-    for h in range(4):
-        weight[h * 128:h * 128 + 64, :] = tall_high[h * 64:(h + 1) * 64]
-        weight[h * 128 + 64:(h + 1) * 128, :] = tall_low[h * 64:(h + 1) * 64]
+    for side in range(2):
+        weight[side * 256:side * 256 + 128, :] = tall_high[side * 128:(side + 1) * 128]
+        weight[side * 256 + 128:(side + 1) * 256, :] = tall_low[side * 128:(side + 1) * 128]
     wide_high, wide_low = halves(tall.T)
     wide[0] = wide_high
     wide[1] = wide_low
 
-    def settle(k, carry):
-        to_near(k, sibling[0]).wait_recv()
-        pass_on(k, far_sibling).wait_recv()
-        return carry
-
-    lax.fori_loop(0, 8, settle, 0)
+    for number in range(4):
+        near_rows(number, 1 - core).wait_recv()
     for copy in load[:2]:
         copy.wait()
     every_wide[...] = every[...].astype(f32)
@@ -303,21 +275,17 @@
     place = jnp.concatenate([wide[0, mine, :], wide[1, mine, :]], axis=0)
     own_mean = mean[mine, :]
     own_sum = rowsum[pl.ds(m, 1), :]
-    ahead_weight = weight[pl.ds(pl.multiple_of(far[0] * 128, 128), 128), :]
-    own_weight = weight[pl.ds(pl.multiple_of(g * 128, 128), 128), :]
+    own_weight = weight[pl.ds(pl.multiple_of(core * 256, 256), 256), :]
 
     def to_sibling(pair, rows):
         here = pl.ds(pair * 256, 256)
         return remote(ratio.at[rows, here], ratio.at[rows, here], ratio_send.at[pair], ratio_recv.at[pair], sibling)
-
-    def over(pair):
-        return remote(ahead.at[pair], from_far.at[pair], sum_send.at[pair], sum_recv.at[pair], far)
 
     def forward(pair):
         columns = []
         for chunk in (2 * pair, 2 * pair + 1):
             columns.append(jnp.concatenate(
-                [every_wide[pl.ds(h * 512 + q * 8 + chunk, 32, stride=16), :] for h in range(4) for q in range(2)], axis=0
+                [every_wide[pl.ds(side * 1024 + q * 8 + chunk, 64, stride=16), :] for side in range(2) for q in range(2)], axis=0
             ))
         both = dot(place, jnp.concatenate(columns, axis=1).astype(bf16))
         value = both[:ROWS] + both[ROWS:]
@@ -331,40 +299,39 @@
             ratio[mine, here] = rest.astype(bf16)
         to_sibling(pair, mine).start()
 
-    def part_of(weights, pair):
-        both = dot(weights, ratio[:, pair * 256:(pair + 1) * 256])
-        return both[:64] + both[64:]
-
-    def send_over(pair):
+    def collect(pair):
         to_sibling(pair, other).wait_recv()
-        ahead[pair] = part_of(ahead_weight, pair).astype(bf16)
-        over(pair).start()
+        both = dot(own_weight, ratio[:, pair * 256:(pair + 1) * 256])
+        value = both[:128] + both[128:]
+        for q in range(2):
+            for side in range(2):
+                straight[pl.ds(q * 8 + 2 * pair + side, 64, stride=16), :] = value[q * 64:(q + 1) * 64, side * LANES:(side + 1) * LANES]
 
     forward(0)
     for pair in range(1, 4):
         forward(pair)
-        send_over(pair - 1)
-    send_over(3)
-    for pair in range(4):
-        own[:, pair * 256:(pair + 1) * 256] = part_of(own_weight, pair)
-    for pair in range(4):
-        over(pair).wait_recv()
-        value = own[:, pair * 256:(pair + 1) * 256] + from_far[pair].astype(f32)
-        for q in range(2):
-            for side in range(2):
-                straight[pl.ds(q * 8 + 2 * pair + side, 32, stride=16), :] = value[q * 32:(q + 1) * 32, side * LANES:(side + 1) * LANES]
-    linear[...] = straight[...].astype(bf16)
-
-    def last_copy(d, member):
-        device = partner(d)
-        return remote(linear.at[slot(0, device[1])], arrived.at[slot(0, member)], out_send.at[d], out_recv.at[d], device)
-
-    def give(d, carry):
-        last_copy(d, m).start()
-        return carry
-
-    lax.fori_loop(1, 32, give, 0)
-    arrived[slot(0, m)] = linear[slot(0, m)]
+        collect(pair - 1)
+    collect(3)
+
+    def slot_of(i):
+        dy, dz, dx = spread_out(i)
+        return ((y + dy) % 4) * 16 + ((z + dz) % 4) * 4 + (x + dx) % 4
+
+    def last_copy(i, number):
+        return remote(
+            linear.at[slot(slot_of(i))], arrived.at[slot(number)], out_send.at[i], out_recv.at[i], partner(i)
+        )
+
+    arrival = (y % 2) * 32 + m
+
+    def give(i, carry):
+        rows = slot(slot_of(i))
+        linear[rows] = straight[rows].astype(bf16)
+        last_copy(i, arrival).start()
+        return carry
+
+    lax.fori_loop(0, 63, give, 0)
+    arrived[slot(arrival)] = straight[slot(here_chip)].astype(bf16)
 
     sine_row = sines(subset, lax.broadcasted_iota(jnp.int32, (8, LANES), 1) % ANGLES)[:1]
     for part in range(PARTS):
@@ -374,40 +341,32 @@
         high = value.astype(bf16).astype(f32)
         depth[part * block:(part + 1) * block, :] = jnp.where(lane < 2 * ANGLES, high, value - high).astype(bf16)
 
-    def sent(d, carry):
-        first_copy(d, partner(d)[0], m).wait_send()
-        first_aux(d, partner(d)[0], m).wait_send()
-        return carry
-
-    lax.fori_loop(1, 32, sent, 0)
-
-    def sent_runs(k, carry):
-        to_far(k, g).wait_send()
-        to_near(k, g).wait_send()
-        pass_on(k, far[0]).wait_send()
-        return carry
-
-    lax.fori_loop(0, 8, sent_runs, 0)
-    aux_copy(0, g, far).wait_send()
-    aux_copy(1, g, sibling).wait_send()
-    aux_copy(2, far[0], sibling).wait_send()
-    for pair in range(4):
-        to_sibling(pair, mine).wait_send()
-        over(pair).wait_send()
+    def sent(i, carry):
+        first_copy(i, here_chip).wait_send()
+        first_aux(i, here_chip).wait_send()
+        return carry
+
+    lax.fori_loop(0, 63, sent, 0)
+    near_aux(core).wait_send()
+    for number in range(4):
+        near_rows(number, core).wait_send()
+        to_sibling(number, mine).wait_send()
     load[2].wait()
 
-    def take(d, carry):
-        last_copy(d, source(d)).wait_recv()
-        return carry
-
-    lax.fori_loop(1, 32, take, 0)
+    def take(i, carry):
+        dy, dz, dx = spread_out(i)
+        y2, z2, x2 = (y + 4 - dy) % 4, (z + 4 - dz) % 4, (x + 4 - dx) % 4
+        last_copy(i, (y2 % 2) * 32 + (y2 // 2) * 16 + z2 * 4 + x2).wait_recv()
+        return carry
+
+    lax.fori_loop(0, 63, take, 0)
     back[...] = arrived[...]
 
-    def given(d, carry):
-        last_copy(d, m).wait_send()
-        return carry
-
-    lax.fori_loop(1, 32, given, 0)
+    def given(i, carry):
+        last_copy(i, arrival).wait_send()
+        return carry
+
+    lax.fori_loop(0, 63, given, 0)
 
 
 def final_kernel(moved, depth, back, volume, scale, residual_in, new_volume, residual, straight, spread, staged, sems, rest_sem):
@@ -415,7 +374,7 @@
     block = DEPTH // PARTS
     keep = pltpu.make_async_copy(residual_in, residual, rest_sem)
     keep.start()
-    straight[...] = back[...].astype(f32)
+    straight[...] = back[:512].astype(f32) + back[512:].astype(f32)
     shift = moved[...]
     copies = []
     for q in range(2):
@@ -450,7 +409,7 @@
         in_specs=[hbm] * 8,
         out_specs=(vmem,) * 6,
         out_shape=(
-            jax.ShapeDtypeStruct((512, LANES), bf16), jax.ShapeDtypeStruct((lines, LANES), f32),
+            jax.ShapeDtypeStruct((1024, LANES), bf16), jax.ShapeDtypeStruct((lines, LANES), f32),
             jax.ShapeDtypeStruct(volume.shape, f32), jax.ShapeDtypeStruct(volume.shape, f32),
             jax.ShapeDtypeStruct((ANGLES, LANES), f32), jax.ShapeDtypeStruct((DEPTH, LANES), bf16),
         ),
@@ -458,15 +417,13 @@
             pltpu.SMEM((ANGLES,), jnp.int32), pltpu.VMEM((ANGLES, 4 * ANGLES), jnp.int32),
             pltpu.VMEM((6, LANES), jnp.int32), pltpu.VMEM((2, FOOT, ANGLES), f32),
             pltpu.VMEM((lines, LANES), f32), pltpu.VMEM((lines, LANES), f32),
-            pltpu.VMEM((ANGLES, CELLS), f32), pltpu.VMEM((512, LANES), f32), pltpu.VMEM((512, LANES), bf16),
+            pltpu.VMEM((ANGLES, CELLS), f32), pltpu.VMEM((1024, LANES), f32), pltpu.VMEM((512, LANES), bf16),
             pltpu.VMEM((ANGLES, 1, LANES), f32), pltpu.VMEM((2048, LANES), bf16), pltpu.VMEM((128, 1, LANES), f32),
             pltpu.VMEM((2048, LANES), f32), pltpu.VMEM((512, 2 * ROWS), bf16), pltpu.VMEM((2, 2 * ROWS, 256), bf16),
             pltpu.VMEM((2 * ROWS, LANES), f32), pltpu.VMEM((2 * ROWS, CELLS), bf16),
-            pltpu.VMEM((4, 64, 256), bf16), pltpu.VMEM((4, 64, 256), bf16), pltpu.VMEM((64, CELLS), f32),
-            pltpu.VMEM((512, LANES), bf16), pltpu.VMEM((512, LANES), bf16),
-            dma((2 * PARTS,)), dma((4,)), dma((3,)), dma((32,)), dma((32,)), dma((32,)), dma((32,)), dma((8,)), dma((8,)),
-            dma((8,)), dma((8,)), dma((8,)), dma((8,)), dma((3,)), dma((3,)), dma((4,)), dma((4,)),
-            dma((4,)), dma((4,)), dma((32,)), dma((32,)),
+            pltpu.VMEM((1024, LANES), bf16), pltpu.VMEM((1024, LANES), bf16),
+            dma((2 * PARTS,)), dma((4,)), dma((3,)), dma((63,)), dma((63,)), dma((63,)), dma((63,)),
+            dma((4,)), dma((4,)), dma((1,)), dma((1,)), dma((4,)), dma((4,)), dma((63,)), dma((63,)),
         ],
         compiler_params=pltpu.CompilerParams(collective_id=0, has_side_effects=True, vmem_limit_bytes=28 << 20),
         cost_estimate=pl.CostEstimate(flops=10 ** 9, bytes_accessed=100 << 20, transcendentals=0),

time: 43.4 us -> 40.6 us (0.935)
  Pallas kernels: 42.6 us -> 39.8 us
    pallas_call x1, Pallas kernels: 39.4 us -> 36.6 us  [shards(): pl.pallas_call(main_kernel, in_specs=[hbm] * 8, out_specs=(vmem,) * 6, ou...]
where the time goes in v4:
time: 40.6 us; the launch traced here: 40.5 us
  Pallas kernels  39.8 us (98%)
  between operations  0.64 us (2%)
    pallas_call x1, Pallas kernels, shards(): pl.pallas_call(main_kernel, in_specs=[hbm] * 8, out_specs=(vmem,) * 6, ou...  36.6 us
    pallas_call x1, Pallas kernels, shards(): pl.pallas_call(final_kernel, in_specs=[vmem, vmem, vmem, vmem, vmem, pl.B...  3.2 us

profile of v4, /device:TPU:1, one launch (start us, length us, event | category | flops | bytes accessed | tf_op | source)
XLA Modules:
  0.0 40.5 jit_solution(3715772814043652110)
XLA Ops:
  0.6 36.6 %exchange.1 = (bf16[1024,128]{1,0:T(8,128)(2,1)S(1)}, f32[1536,128]{1,0:T(8,128)S(1)}, f32[2,768,768]{2,1,0:T(8,128)S(1)}, f32[2,768,768]{2,1,0:T(8,128)S(1)}, f...) custom-call(s32[32]{0:T(128)} %subset_hbm.1, s32[32,128]{1,0:T(8,128)} %row_start_hbm.1, s32[6,128]{1,0:T(8,128)} %bitcast.8, ...), custom_call_target="tpu_custom_call" | custom-call | flops 1000000000 | bytes 104857600 | tf_op jit(solution)/shard_map/exchange/pallas_call | solution.py:407
  37.3 3.2 %final.1 = (f32[2,768,768]{2,1,0:T(8,128)}, f32[1536,128]{1,0:T(8,128)}) custom-call(f32[32,128]{1,0:T(8,128)S(1)} %get-tuple-element.10.moved, bf16[768,128]{1,0:T(8,128)(2,1)S(1)} %get-tuple-element.11.depth, bf16[1024,128]{1,0:T(8,128)(2,1)S(1)} %get-tuple-element.12.back, f32[2,768,768]{2,1,0:T(8,128)S(1)} %get-tuple-element.13.volume, ...), custom_call_target="tpu_custom_call" | custom-call | flops 226492416 | bytes 14155776 | tf_op jit(solution)/shard_map/final/pallas_call | solution.py:437

commit v5 on v4

--- a/solution.py
+++ b/solution.py
@@ -1,3 +1,4 @@
+import itertools
 import math
 
 import jax
@@ -17,6 +18,9 @@
 CELLS = 1024
 ROWS = 192
 PARTS = 3
+OFFSETS = sorted(
+    itertools.product(range(4), repeat=3), key=lambda offset: -sum(min(step, 4 - step) for step in offset)
+)[:-1]
 STEP = 0.8 * CELLS / COLS
 
 
@@ -107,20 +111,19 @@
     y, z, x = (m // 16) * 2 + g // 2, (m // 4) % 4, m % 4
     sibling = (g - core + (1 - core), m)
 
-    def chip(y, z, x):
-        return (y % 2) * 2 + core, (y // 2) * 16 + z * 4 + x
-
-    def spread_out(i):
-        far_first = lambda j: jnp.where(j == 0, 2, jnp.where(j == 1, 1, jnp.where(j == 2, 3, 0)))
-        return far_first(i // 16), far_first((i // 4) % 4), far_first(i % 4)
-
-    def partner(i):
-        dy, dz, dx = spread_out(i)
-        return chip((y + dy) % 4, (z + dz) % 4, (x + dx) % 4)
-
-    def source(i):
-        dy, dz, dx = spread_out(i)
-        return ((y + 4 - dy) % 4) * 16 + ((z + 4 - dz) % 4) * 4 + (x + 4 - dx) % 4
+    ys, zs, xs = ([(place + step) % 4 for step in range(4)] for place in (y, z, x))
+    group_of = [place % 2 * 2 + core for place in ys]
+    plane_of = [place // 2 * 16 for place in ys]
+    line_of = [[row * 4 + col for col in xs] for row in zs]
+
+    def partner(offset):
+        return group_of[offset[0]], plane_of[offset[0]] + line_of[offset[1]][offset[2]]
+
+    def partner_slot(offset):
+        return ys[offset[0]] * 16 + line_of[offset[1]][offset[2]]
+
+    def arrived_all(ref, sem):
+        return pltpu.make_async_copy(ref, ref, sem)
 
     here_chip = y * 16 + z * 4 + x
 
@@ -155,11 +158,8 @@
     ]
     barrier = pltpu.get_barrier_semaphore()
 
-    def greet(d, carry):
-        pl.semaphore_signal(barrier, inc=1, device_id=partner(d), device_id_type=MESH)
-        return carry
-
-    lax.fori_loop(0, 63, greet, 0)
+    for offset in OFFSETS:
+        pl.semaphore_signal(barrier, inc=1, device_id=partner(offset), device_id_type=MESH)
     pl.semaphore_signal(barrier, inc=1, device_id=sibling, device_id_type=MESH)
 
     for copy in small:
@@ -200,43 +200,30 @@
 
     pl.semaphore_wait(barrier, 64)
 
-    def first_copy(i, number):
-        device = partner(i)
-        return remote(sino.at[slot(device[1])], every.at[slot(core * 64 + number)], send_sem.at[i], recv_sem.at[i], device)
-
-    def first_aux(i, number):
-        device = partner(i)
-        return remote(aux.at[device[1]], every_aux.at[core * 64 + number], aux_send.at[i], aux_recv.at[i], device)
-
-    def send(i, carry):
-        first_aux(i, here_chip).start()
-        first_copy(i, here_chip).start()
-        return carry
-
-    lax.fori_loop(0, 63, send, 0)
+    for offset in OFFSETS:
+        device = partner(offset)
+        remote(
+            aux.at[device[1]], every_aux.at[core * 64 + here_chip], aux_send.at[0], aux_recv.at[0], device
+        ).start()
+        remote(
+            sino.at[slot(device[1])], every.at[slot(core * 64 + here_chip)], send_sem.at[0], recv_sem.at[offset[0]], device
+        ).start()
     every[slot(core * 64 + here_chip)] = sino[slot(m)]
     every_aux[core * 64 + here_chip] = aux[m]
 
     def near_rows(number, side):
-        rows = slot(side * 64 + ((y + 4 - number) % 4) * 16, 16)
+        rows = slot(side * 64 + ys[(4 - number) % 4] * 16, 16)
         return remote(every.at[rows], every.at[rows], near_send.at[number], near_recv.at[number], sibling)
 
     def near_aux(side):
         rows = pl.ds(side * 64, 64)
         return remote(every_aux.at[rows], every_aux.at[rows], aux2_send.at[0], aux2_recv.at[0], sibling)
 
-    def arrive_aux(i, carry):
-        first_aux(i, source(i)).wait_recv()
-        return carry
-
-    def arrive(i, carry):
-        first_copy(i, source(i)).wait_recv()
-        return carry
-
-    lax.fori_loop(0, 63, arrive_aux, 0)
+    arrived_all(every_aux.at[pl.ds(core * 64, 63)], aux_recv.at[0]).wait()
     near_aux(core).start()
-    for number, order_of in ((0, 3), (1, 1), (3, 2), (2, 0)):
-        lax.fori_loop(order_of * 16, order_of * 16 + (15 if number == 0 else 16), arrive, 0)
+    for number in (0, 1, 3, 2):
+        rows = slot(core * 64 + ys[(4 - number) % 4] * 16, 15 if number == 0 else 16)
+        arrived_all(every.at[rows], recv_sem.at[number]).wait()
         near_rows(number, core).start()
     near_aux(1 - core).wait_recv()
 
@@ -313,24 +300,11 @@
         collect(pair - 1)
     collect(3)
 
-    def slot_of(i):
-        dy, dz, dx = spread_out(i)
-        return ((y + dy) % 4) * 16 + ((z + dz) % 4) * 4 + (x + dx) % 4
-
-    def last_copy(i, number):
-        return remote(
-            linear.at[slot(slot_of(i))], arrived.at[slot(number)], out_send.at[i], out_recv.at[i], partner(i)
-        )
-
     arrival = (y % 2) * 32 + m
-
-    def give(i, carry):
-        rows = slot(slot_of(i))
+    for offset in OFFSETS:
+        rows = slot(partner_slot(offset))
         linear[rows] = straight[rows].astype(bf16)
-        last_copy(i, arrival).start()
-        return carry
-
-    lax.fori_loop(0, 63, give, 0)
+        remote(linear.at[rows], arrived.at[slot(arrival)], out_send.at[0], out_recv.at[0], partner(offset)).start()
     arrived[slot(arrival)] = straight[slot(here_chip)].astype(bf16)
 
     sine_row = sines(subset, lax.broadcasted_iota(jnp.int32, (8, LANES), 1) % ANGLES)[:1]
@@ -341,32 +315,17 @@
         high = value.astype(bf16).astype(f32)
         depth[part * block:(part + 1) * block, :] = jnp.where(lane < 2 * ANGLES, high, value - high).astype(bf16)
 
-    def sent(i, carry):
-        first_copy(i, here_chip).wait_send()
-        first_aux(i, here_chip).wait_send()
-        return carry
-
-    lax.fori_loop(0, 63, sent, 0)
+    arrived_all(every.at[slot(0, 63)], send_sem.at[0]).wait()
+    arrived_all(every_aux.at[pl.ds(0, 63)], aux_send.at[0]).wait()
     near_aux(core).wait_send()
     for number in range(4):
         near_rows(number, core).wait_send()
         to_sibling(number, mine).wait_send()
     load[2].wait()
 
-    def take(i, carry):
-        dy, dz, dx = spread_out(i)
-        y2, z2, x2 = (y + 4 - dy) % 4, (z + 4 - dz) % 4, (x + 4 - dx) % 4
-        last_copy(i, (y2 % 2) * 32 + (y2 // 2) * 16 + z2 * 4 + x2).wait_recv()
-        return carry
-
-    lax.fori_loop(0, 63, take, 0)
+    arrived_all(arrived.at[slot(0, 63)], out_recv.at[0]).wait()
     back[...] = arrived[...]
-
-    def given(i, carry):
-        last_copy(i, arrival).wait_send()
-        return carry
-
-    lax.fori_loop(0, 63, given, 0)
+    arrived_all(linear.at[slot(0, 63)], out_send.at[0]).wait()
 
 
 def final_kernel(moved, depth, back, volume, scale, residual_in, new_volume, residual, straight, spread, staged, sems, rest_sem):
@@ -422,8 +381,8 @@
             pltpu.VMEM((2048, LANES), f32), pltpu.VMEM((512, 2 * ROWS), bf16), pltpu.VMEM((2, 2 * ROWS, 256), bf16),
             pltpu.VMEM((2 * ROWS, LANES), f32), pltpu.VMEM((2 * ROWS, CELLS), bf16),
             pltpu.VMEM((1024, LANES), bf16), pltpu.VMEM((1024, LANES), bf16),
-            dma((2 * PARTS,)), dma((4,)), dma((3,)), dma((63,)), dma((63,)), dma((63,)), dma((63,)),
-            dma((4,)), dma((4,)), dma((1,)), dma((1,)), dma((4,)), dma((4,)), dma((63,)), dma((63,)),
+            dma((2 * PARTS,)), dma((4,)), dma((3,)), dma((1,)), dma((4,)), dma((1,)), dma((1,)),
+            dma((4,)), dma((4,)), dma((1,)), dma((1,)), dma((4,)), dma((4,)), dma((1,)), dma((1,)),
         ],
         compiler_params=pltpu.CompilerParams(collective_id=0, has_side_effects=True, vmem_limit_bytes=28 << 20),
         cost_estimate=pl.CostEstimate(flops=10 ** 9, bytes_accessed=100 << 20, transcendentals=0),

time: 40.6 us -> 35.2 us (0.87)
  Pallas kernels: 39.8 us -> 34.5 us
    pallas_call x1, Pallas kernels: 36.6 us -> 31.3 us  [shards(): pl.pallas_call(main_kernel, in_specs=[hbm] * 8, out_specs=(vmem,) * 6, ou...]
where the time goes in v5:
time: 35.2 us; the launch traced here: 35.1 us
  Pallas kernels  34.5 us (98%)
  between operations  0.64 us (2%)
    pallas_call x1, Pallas kernels, shards(): pl.pallas_call(main_kernel, in_specs=[hbm] * 8, out_specs=(vmem,) * 6, ou...  31.3 us
    pallas_call x1, Pallas kernels, shards(): pl.pallas_call(final_kernel, in_specs=[vmem, vmem, vmem, vmem, vmem, pl.B...  3.2 us

profile of v5, /device:TPU:1, one launch (start us, length us, event | category | flops | bytes accessed | tf_op | source)
XLA Modules:
  0.0 35.1 jit_solution(8660102938295485677)
XLA Ops:
  0.6 31.3 %exchange.1 = (bf16[1024,128]{1,0:T(8,128)(2,1)S(1)}, f32[1536,128]{1,0:T(8,128)S(1)}, f32[2,768,768]{2,1,0:T(8,128)S(1)}, f32[2,768,768]{2,1,0:T(8,128)S(1)}, f...) custom-call(s32[32]{0:T(128)} %subset_hbm.1, s32[32,128]{1,0:T(8,128)} %row_start_hbm.1, s32[6,128]{1,0:T(8,128)} %bitcast.8, ...), custom_call_target="tpu_custom_call" | custom-call | flops 1000000000 | bytes 104857600 | tf_op jit(solution)/shard_map/exchange/pallas_call | solution.py:366
  31.9 3.2 %final.1 = (f32[2,768,768]{2,1,0:T(8,128)}, f32[1536,128]{1,0:T(8,128)}) custom-call(f32[32,128]{1,0:T(8,128)S(1)} %get-tuple-element.10.moved, bf16[768,128]{1,0:T(8,128)(2,1)S(1)} %get-tuple-element.11.depth, bf16[1024,128]{1,0:T(8,128)(2,1)S(1)} %get-tuple-element.12.back, f32[2,768,768]{2,1,0:T(8,128)S(1)} %get-tuple-element.13.volume, ...), custom_call_target="tpu_custom_call" | custom-call | flops 226492416 | bytes 14155776 | tf_op jit(solution)/shard_map/final/pallas_call | solution.py:396

commit v6 on v5

--- a/solution.py
+++ b/solution.py
@@ -99,10 +99,10 @@
 def main_kernel(
     subset_hbm, row_start_hbm, order_hbm, axial_hbm, volume_hbm, scale_hbm, measured_hbm, norm_hbm,
     back, residual, volume, scale, moved, depth,
-    subset, row_start, order, axial, measured, norm, rowsum, straight, sino, aux, every, every_aux, every_wide, weight, wide, mean,
-    ratio, linear, arrived,
+    subset, row_start, order, axial, measured, norm, rowsum, straight, sino, aux, every, every_aux, every_wide, tall, weight, wide, mean,
+    ratio, partial, from_sibling, linear, arrived,
     volume_sem, small_sem, load_sem, send_sem, recv_sem, aux_send, aux_recv,
-    near_send, near_recv, aux2_send, aux2_recv, ratio_send, ratio_recv, out_send, out_recv,
+    sum_send, sum_recv, ratio_send, ratio_recv, out_send, out_recv,
 ):
     f32, bf16 = jnp.float32, jnp.bfloat16
     block = DEPTH // PARTS
@@ -203,102 +203,94 @@
     for offset in OFFSETS:
         device = partner(offset)
         remote(
-            aux.at[device[1]], every_aux.at[core * 64 + here_chip], aux_send.at[0], aux_recv.at[0], device
+            aux.at[device[1]], every_aux.at[here_chip], aux_send.at[0], aux_recv.at[offset[0]], device
         ).start()
         remote(
-            sino.at[slot(device[1])], every.at[slot(core * 64 + here_chip)], send_sem.at[0], recv_sem.at[offset[0]], device
+            sino.at[slot(device[1])], every.at[slot(here_chip)], send_sem.at[0], recv_sem.at[offset[0]], device
         ).start()
-    every[slot(core * 64 + here_chip)] = sino[slot(m)]
-    every_aux[core * 64 + here_chip] = aux[m]
-
-    def near_rows(number, side):
-        rows = slot(side * 64 + ys[(4 - number) % 4] * 16, 16)
-        return remote(every.at[rows], every.at[rows], near_send.at[number], near_recv.at[number], sibling)
-
-    def near_aux(side):
-        rows = pl.ds(side * 64, 64)
-        return remote(every_aux.at[rows], every_aux.at[rows], aux2_send.at[0], aux2_recv.at[0], sibling)
-
-    arrived_all(every_aux.at[pl.ds(core * 64, 63)], aux_recv.at[0]).wait()
-    near_aux(core).start()
-    for number in (0, 1, 3, 2):
-        rows = slot(core * 64 + ys[(4 - number) % 4] * 16, 15 if number == 0 else 16)
-        arrived_all(every.at[rows], recv_sem.at[number]).wait()
-        near_rows(number, core).start()
-    near_aux(1 - core).wait_recv()
-
-    table = every_aux[...].reshape(4 * ANGLES, LANES)
+    every[slot(here_chip)] = sino[slot(m)]
+    every_aux[here_chip] = aux[m]
+
     rows = order[...].astype(f32)
     lower = jnp.concatenate([rows[i:i + 1] for i in range(3)], axis=1)
     upper = jnp.concatenate([rows[i:i + 1] for i in range(3, 6)], axis=1)
-    offset = jnp.where(y % 2 == 0, lower, upper) - table[:, 16:17]
-    tall, level = [None] * 4, [None] * 4
-    for q in range(2):
-        value = jnp.zeros_like(offset)
-        for r in range(FOOT):
-            value = jnp.where(offset == float(r), table[:, q * FOOT + r:q * FOOT + r + 1], value)
-        for side in range(2):
-            tall[side * 2 + q] = value[side * 64:(side + 1) * 64]
-            level[side * 2 + q] = table[side * 64:(side + 1) * 64, 17 + q:18 + q]
-    tall, level = jnp.concatenate(tall, axis=0), jnp.concatenate(level, axis=0)
-    constant = jnp.sum(tall * level, axis=0, keepdims=True)
-    mean[...] = jnp.broadcast_to(constant, (LANES, 2 * ROWS)).T
-    tall_high, tall_low = halves(tall)
-    for side in range(2):
-        weight[side * 256:side * 256 + 128, :] = tall_high[side * 128:(side + 1) * 128]
-        weight[side * 256 + 128:(side + 1) * 256, :] = tall_low[side * 128:(side + 1) * 128]
-    wide_high, wide_low = halves(tall.T)
-    wide[0] = wide_high
-    wide[1] = wide_low
-
-    for number in range(4):
-        near_rows(number, 1 - core).wait_recv()
+    rows = jnp.where(y % 2 == 0, lower, upper)
+    constant = 0.0
+    for number in (0, 1, 3, 2):
+        low, count = pl.multiple_of(ys[(4 - number) % 4] * 16, 16), 15 if number == 0 else 16
+        arrived_all(every_aux.at[pl.ds(low, count)], aux_recv.at[number]).wait()
+        table = every_aux[pl.ds(low, 16)].reshape(16, LANES)
+        offset = rows - table[:, 16:17]
+        for q in range(2):
+            value = jnp.zeros_like(offset)
+            for r in range(FOOT):
+                value = jnp.where(offset == float(r), table[:, q * FOOT + r:q * FOOT + r + 1], value)
+            tall[pl.ds(q * 64 + low, 16), :] = value
+            constant = constant + jnp.sum(value * table[:, 17 + q:18 + q], axis=0, keepdims=True)
+        arrived_all(every.at[slot(low, count)], recv_sem.at[number]).wait()
+        every_wide[slot(low, 16), :] = every[slot(low, 16), :].astype(f32)
+    own_mean = jnp.broadcast_to(constant, (LANES, 2 * ROWS)).T
+    tall_high, tall_low = halves(tall[...])
+    weight[0:128, :] = tall_high
+    weight[128:256, :] = tall_low
+    wide_high, wide_low = halves(tall[...].T)
+    wide[:, 0:128] = wide_high
+    wide[:, 128:256] = wide_low
     for copy in load[:2]:
         copy.wait()
-    every_wide[...] = every[...].astype(f32)
 
     mine = pl.ds(pl.multiple_of(core * ROWS, ROWS), ROWS)
     other = pl.ds(pl.multiple_of((1 - core) * ROWS, ROWS), ROWS)
-    place = jnp.concatenate([wide[0, mine, :], wide[1, mine, :]], axis=0)
-    own_mean = mean[mine, :]
+    mean[...] = own_mean
     own_sum = rowsum[pl.ds(m, 1), :]
-    own_weight = weight[pl.ds(pl.multiple_of(core * 256, 256), 256), :]
 
     def to_sibling(pair, rows):
         here = pl.ds(pair * 256, 256)
         return remote(ratio.at[rows, here], ratio.at[rows, here], ratio_send.at[pair], ratio_recv.at[pair], sibling)
 
+    def half_sums(pair):
+        return remote(partial.at[pair, other], from_sibling.at[pair], sum_send.at[pair], sum_recv.at[pair], sibling)
+
     def forward(pair):
-        columns = []
-        for chunk in (2 * pair, 2 * pair + 1):
-            columns.append(jnp.concatenate(
-                [every_wide[pl.ds(side * 1024 + q * 8 + chunk, 64, stride=16), :] for side in range(2) for q in range(2)], axis=0
-            ))
-        both = dot(place, jnp.concatenate(columns, axis=1).astype(bf16))
-        value = both[:ROWS] + both[ROWS:]
+        columns = jnp.concatenate([
+            jnp.concatenate([every_wide[pl.ds(q * 8 + chunk, 64, stride=16), :] for q in range(2)], axis=0)
+            for chunk in (2 * pair, 2 * pair + 1)
+        ], axis=1).astype(bf16)
+        value = dot(wide[...], jnp.concatenate([columns, columns], axis=0))
+        for side in range(2):
+            here = slice((2 * pair + side) * LANES, (2 * pair + side + 1) * LANES)
+            partial[pair, :, side * LANES:(side + 1) * LANES] = (
+                value[:, side * LANES:(side + 1) * LANES] + mean[...] * own_sum[:, here]
+            )
+        half_sums(pair).start()
+
+    def finish(pair):
+        half_sums(pair).wait_recv()
         for side in range(2):
             chunk = 2 * pair + side
-            here = slice(chunk * LANES, (chunk + 1) * LANES)
-            found = value[:, side * LANES:(side + 1) * LANES] + own_mean * own_sum[:, here]
+            here = slice(side * LANES, (side + 1) * LANES)
+            found = partial[pair, mine, here] + from_sibling[pair, :, here]
             rows = pl.ds(chunk, ROWS, stride=8)
             rest = norm[rows, :] * (measured[rows, :] - found)
             residual[rows, :] = rest
-            ratio[mine, here] = rest.astype(bf16)
+            ratio[mine, chunk * LANES:(chunk + 1) * LANES] = rest.astype(bf16)
         to_sibling(pair, mine).start()
 
     def collect(pair):
         to_sibling(pair, other).wait_recv()
-        both = dot(own_weight, ratio[:, pair * 256:(pair + 1) * 256])
+        both = dot(weight[...], ratio[:, pair * 256:(pair + 1) * 256])
         value = both[:128] + both[128:]
         for q in range(2):
             for side in range(2):
                 straight[pl.ds(q * 8 + 2 * pair + side, 64, stride=16), :] = value[q * 64:(q + 1) * 64, side * LANES:(side + 1) * LANES]
 
-    forward(0)
-    for pair in range(1, 4):
-        forward(pair)
-        collect(pair - 1)
-    collect(3)
+    for step in range(6):
+        if step < 4:
+            forward(step)
+        if 0 <= step - 1 < 4:
+            finish(step - 1)
+        if 0 <= step - 2 < 4:
+            collect(step - 2)
 
     arrival = (y % 2) * 32 + m
     for offset in OFFSETS:
@@ -317,9 +309,8 @@
 
     arrived_all(every.at[slot(0, 63)], send_sem.at[0]).wait()
     arrived_all(every_aux.at[pl.ds(0, 63)], aux_send.at[0]).wait()
-    near_aux(core).wait_send()
     for number in range(4):
-        near_rows(number, core).wait_send()
+        half_sums(number).wait_send()
         to_sibling(number, mine).wait_send()
     load[2].wait()
 
@@ -377,12 +368,13 @@
             pltpu.VMEM((6, LANES), jnp.int32), pltpu.VMEM((2, FOOT, ANGLES), f32),
             pltpu.VMEM((lines, LANES), f32), pltpu.VMEM((lines, LANES), f32),
             pltpu.VMEM((ANGLES, CELLS), f32), pltpu.VMEM((1024, LANES), f32), pltpu.VMEM((512, LANES), bf16),
-            pltpu.VMEM((ANGLES, 1, LANES), f32), pltpu.VMEM((2048, LANES), bf16), pltpu.VMEM((128, 1, LANES), f32),
-            pltpu.VMEM((2048, LANES), f32), pltpu.VMEM((512, 2 * ROWS), bf16), pltpu.VMEM((2, 2 * ROWS, 256), bf16),
-            pltpu.VMEM((2 * ROWS, LANES), f32), pltpu.VMEM((2 * ROWS, CELLS), bf16),
+            pltpu.VMEM((ANGLES, 1, LANES), f32), pltpu.VMEM((1024, LANES), bf16), pltpu.VMEM((64, 1, LANES), f32),
+            pltpu.VMEM((1024, LANES), f32), pltpu.VMEM((128, 2 * ROWS), f32), pltpu.VMEM((256, 2 * ROWS), bf16),
+            pltpu.VMEM((2 * ROWS, 256), bf16), pltpu.VMEM((2 * ROWS, LANES), f32), pltpu.VMEM((2 * ROWS, CELLS), bf16),
+            pltpu.VMEM((4, 2 * ROWS, 256), f32), pltpu.VMEM((4, ROWS, 256), f32),
             pltpu.VMEM((1024, LANES), bf16), pltpu.VMEM((1024, LANES), bf16),
-            dma((2 * PARTS,)), dma((4,)), dma((3,)), dma((1,)), dma((4,)), dma((1,)), dma((1,)),
-            dma((4,)), dma((4,)), dma((1,)), dma((1,)), dma((4,)), dma((4,)), dma((1,)), dma((1,)),
+            dma((2 * PARTS,)), dma((4,)), dma((3,)), dma((1,)), dma((4,)), dma((1,)), dma((4,)),
+            dma((4,)), dma((4,)), dma((4,)), dma((4,)), dma((1,)), dma((1,)),
         ],
         compiler_params=pltpu.CompilerParams(collective_id=0, has_side_effects=True, vmem_limit_bytes=28 << 20),
         cost_estimate=pl.CostEstimate(flops=10 ** 9, bytes_accessed=100 << 20, transcendentals=0),

time: 35.2 us -> 33.8 us (0.960); the launches traced: 35.1 us -> 33.3 us
  Pallas kernels: 34.5 us -> 32.6 us
    pallas_call x1, Pallas kernels: 31.3 us -> 29.4 us  [shards(): pl.pallas_call(main_kernel, in_specs=[hbm] * 8, out_specs=(vmem,) * 6, ou...]
where the time goes in v6:
time: 33.8 us; the launch traced here: 33.3 us
  Pallas kernels  32.6 us (96%)
  between operations  0.64 us (2%)
    pallas_call x1, Pallas kernels, shards(): pl.pallas_call(main_kernel, in_specs=[hbm] * 8, out_specs=(vmem,) * 6, ou...  29.4 us
    pallas_call x1, Pallas kernels, shards(): pl.pallas_call(final_kernel, in_specs=[vmem, vmem, vmem, vmem, vmem, pl.B...  3.2 us

profile of v6, /device:TPU:1, one launch (start us, length us, event | category | flops | bytes accessed | tf_op | source)
XLA Modules:
  0.0 33.3 jit_solution(1736383664181913109)
XLA Ops:
  0.6 29.4 %exchange.1 = (bf16[1024,128]{1,0:T(8,128)(2,1)S(1)}, f32[1536,128]{1,0:T(8,128)S(1)}, f32[2,768,768]{2,1,0:T(8,128)S(1)}, f32[2,768,768]{2,1,0:T(8,128)S(1)}, f...) custom-call(s32[32]{0:T(128)} %subset_hbm.1, s32[32,128]{1,0:T(8,128)} %row_start_hbm.1, s32[6,128]{1,0:T(8,128)} %bitcast.8, ...), custom_call_target="tpu_custom_call" | custom-call | flops 1000000000 | bytes 104857600 | tf_op jit(solution)/shard_map/exchange/pallas_call | solution.py:357
  30.1 3.2 %final.1 = (f32[2,768,768]{2,1,0:T(8,128)}, f32[1536,128]{1,0:T(8,128)}) custom-call(f32[32,128]{1,0:T(8,128)S(1)} %get-tuple-element.10.moved, bf16[768,128]{1,0:T(8,128)(2,1)S(1)} %get-tuple-element.11.depth, bf16[1024,128]{1,0:T(8,128)(2,1)S(1)} %get-tuple-element.12.back, f32[2,768,768]{2,1,0:T(8,128)S(1)} %get-tuple-element.13.volume, ...), custom_call_target="tpu_custom_call" | custom-call | flops 226492416 | bytes 14155776 | tf_op jit(solution)/shard_map/final/pallas_call | solution.py:388

commit v7 on v6

--- a/solution.py
+++ b/solution.py
@@ -99,10 +99,10 @@
 def main_kernel(
     subset_hbm, row_start_hbm, order_hbm, axial_hbm, volume_hbm, scale_hbm, measured_hbm, norm_hbm,
     back, residual, volume, scale, moved, depth,
-    subset, row_start, order, axial, measured, norm, rowsum, straight, sino, aux, every, every_aux, every_wide, tall, weight, wide, mean,
-    ratio, partial, from_sibling, linear, arrived,
+    subset, row_start, order, axial, measured, norm, rowsum, straight, sino, aux, every, every_aux, every_wide, tall, weight, wide, matrix,
+    remainder, ratio, linear, arrived,
     volume_sem, small_sem, load_sem, send_sem, recv_sem, aux_send, aux_recv,
-    sum_send, sum_recv, ratio_send, ratio_recv, out_send, out_recv,
+    near_send, near_recv, aux2_send, aux2_recv, input_send, input_recv, out_send, out_recv,
 ):
     f32, bf16 = jnp.float32, jnp.bfloat16
     block = DEPTH // PARTS
@@ -151,11 +151,16 @@
             bring.append(pltpu.make_async_copy(volume_hbm.at[q, here], volume.at[q, here], volume_sem.at[q * PARTS + part]))
     for copy in bring:
         copy.start()
+    mine = pl.ds(pl.multiple_of(core * ROWS, ROWS), ROWS)
+    other = pl.ds(pl.multiple_of((1 - core) * ROWS, ROWS), ROWS)
     load = [
-        pltpu.make_async_copy(measured_hbm, measured, load_sem.at[0]),
-        pltpu.make_async_copy(norm_hbm, norm, load_sem.at[1]),
-        pltpu.make_async_copy(scale_hbm, scale, load_sem.at[2]),
+        pltpu.make_async_copy(
+            array.at[:, chunk, :], target.at[mine, pl.ds(chunk * LANES, LANES)], load_sem.at[number * 8 + chunk]
+        )
+        for number, (array, target) in enumerate(((measured_hbm, measured), (norm_hbm, norm))) for chunk in range(8)
     ]
+    load_scale = pltpu.make_async_copy(scale_hbm, scale, load_sem.at[16])
+
     barrier = pltpu.get_barrier_semaphore()
 
     for offset in OFFSETS:
@@ -183,6 +188,7 @@
         tiles.append([total[:, t * LANES:(t + 1) * LANES] for t in range(COLS // LANES)])
     for copy in load:
         copy.start()
+    load_scale.start()
     for chunk in range(CELLS // LANES):
         values, sums = ray_sums(tiles, shift, chunk)
         rowsum[:, chunk * LANES:(chunk + 1) * LANES] = sums
@@ -203,94 +209,128 @@
     for offset in OFFSETS:
         device = partner(offset)
         remote(
-            aux.at[device[1]], every_aux.at[here_chip], aux_send.at[0], aux_recv.at[offset[0]], device
+            aux.at[device[1]], every_aux.at[core * 64 + here_chip], aux_send.at[0], aux_recv.at[offset[0]], device
         ).start()
         remote(
-            sino.at[slot(device[1])], every.at[slot(here_chip)], send_sem.at[0], recv_sem.at[offset[0]], device
+            sino.at[slot(device[1])], every.at[slot(core * 64 + here_chip)], send_sem.at[0], recv_sem.at[offset[0]], device
         ).start()
-    every[slot(here_chip)] = sino[slot(m)]
-    every_aux[here_chip] = aux[m]
+    every[slot(core * 64 + here_chip)] = sino[slot(m)]
+    every_aux[core * 64 + here_chip] = aux[m]
+
+    for copy in load:
+        copy.wait()
+
+    def near_input(number, rows):
+        target = (measured, norm)[number].at[rows]
+        return remote(target, target, input_send.at[number], input_recv.at[number], sibling)
+
+    near_input(0, mine).start()
+    near_input(1, mine).start()
 
     rows = order[...].astype(f32)
     lower = jnp.concatenate([rows[i:i + 1] for i in range(3)], axis=1)
     upper = jnp.concatenate([rows[i:i + 1] for i in range(3, 6)], axis=1)
     rows = jnp.where(y % 2 == 0, lower, upper)
-    constant = 0.0
-    for number in (0, 1, 3, 2):
-        low, count = pl.multiple_of(ys[(4 - number) % 4] * 16, 16), 15 if number == 0 else 16
-        arrived_all(every_aux.at[pl.ds(low, count)], aux_recv.at[number]).wait()
+    own_sum = rowsum[pl.ds(m, 1), :]
+
+    def first_slot(number, side):
+        return pl.multiple_of(side * 64 + ys[(4 - number) % 4] * 16, 16)
+
+    def near_rows(number, side):
+        here = slot(first_slot(number, side), 16)
+        return remote(every.at[here], every.at[here], near_send.at[number], near_recv.at[number], sibling)
+
+    def near_aux(number, side):
+        here = pl.ds(first_slot(number, side), 16)
+        return remote(every_aux.at[here], every_aux.at[here], aux2_send.at[number], aux2_recv.at[number], sibling)
+
+    def place(step, number, side, turn):
+        low = first_slot(number, side)
         table = every_aux[pl.ds(low, 16)].reshape(16, LANES)
         offset = rows - table[:, 16:17]
+        lane = lax.broadcasted_iota(jnp.int32, (16, LANES), 1)
+        every_wide[...] = every[slot(low, 16), :].astype(f32)
         for q in range(2):
             value = jnp.zeros_like(offset)
             for r in range(FOOT):
                 value = jnp.where(offset == float(r), table[:, q * FOOT + r:q * FOOT + r + 1], value)
-            tall[pl.ds(q * 64 + low, 16), :] = value
-            constant = constant + jnp.sum(value * table[:, 17 + q:18 + q], axis=0, keepdims=True)
+            line = step * 64 + turn * 32 + q * 16
+            tall[line:line + 16, :] = value
+            if turn == 0:
+                high, low_part = halves(value)
+                weight[step * 32 + q * 16:step * 32 + q * 16 + 16, :] = high
+                weight[128 + step * 32 + q * 16:128 + step * 32 + q * 16 + 16, :] = low_part
+            for chunk in range(8):
+                matrix[line:line + 16, chunk * LANES:(chunk + 1) * LANES] = (
+                    every_wide[pl.ds(q * 8 + chunk, 16, stride=16), :].astype(bf16)
+                )
+            high, low_part = halves(table[:, 17 + q:18 + q])
+            level = jnp.where(lane == 0, high.astype(f32), jnp.where(lane == 1, low_part.astype(f32), 0.0))
+            matrix[line:line + 16, CELLS:CELLS + LANES] = level.astype(bf16)
+
+    def own_rows(step, number):
+        low, count = first_slot(number, core), 15 if number == 0 else 16
+        arrived_all(every_aux.at[pl.ds(low, count)], aux_recv.at[number]).wait()
+        near_aux(number, core).start()
         arrived_all(every.at[slot(low, count)], recv_sem.at[number]).wait()
-        every_wide[slot(low, 16), :] = every[slot(low, 16), :].astype(f32)
-    own_mean = jnp.broadcast_to(constant, (LANES, 2 * ROWS)).T
-    tall_high, tall_low = halves(tall[...])
-    weight[0:128, :] = tall_high
-    weight[128:256, :] = tall_low
-    wide_high, wide_low = halves(tall[...].T)
-    wide[:, 0:128] = wide_high
-    wide[:, 128:256] = wide_low
-    for copy in load[:2]:
-        copy.wait()
-
-    mine = pl.ds(pl.multiple_of(core * ROWS, ROWS), ROWS)
-    other = pl.ds(pl.multiple_of((1 - core) * ROWS, ROWS), ROWS)
-    mean[...] = own_mean
-    own_sum = rowsum[pl.ds(m, 1), :]
-
-    def to_sibling(pair, rows):
-        here = pl.ds(pair * 256, 256)
-        return remote(ratio.at[rows, here], ratio.at[rows, here], ratio_send.at[pair], ratio_recv.at[pair], sibling)
-
-    def half_sums(pair):
-        return remote(partial.at[pair, other], from_sibling.at[pair], sum_send.at[pair], sum_recv.at[pair], sibling)
+        near_rows(number, core).start()
+        place(step, number, core, 0)
+
+    def sibling_rows(step, number):
+        near_aux(number, 1 - core).wait_recv()
+        near_rows(number, 1 - core).wait_recv()
+        place(step, number, 1 - core, 1)
+
+    def turn_over(part):
+        high, low = halves(tall[part * LANES:(part + 1) * LANES, :].T)
+        wide[:, part * LANES:(part + 1) * LANES] = high
+        wide[:, 256 + part * LANES:256 + (part + 1) * LANES] = low
+
+    sequence = (0, 1, 3, 2)
+    own_rows(0, 0)
+    own_rows(1, 1)
+    sibling_rows(0, 0)
+    own_rows(2, 3)
+    sibling_rows(1, 1)
+    turn_over(0)
+    near_input(0, other).wait_recv()
+    near_input(1, other).wait_recv()
+    own_rows(3, 2)
+    sibling_rows(2, 3)
+    sibling_rows(3, 2)
+    turn_over(1)
+
+    def product(here):
+        right = matrix[:, here]
+        return dot(wide[...], jnp.concatenate([right, right], axis=0))
+
+    level = product(slice(CELLS, CELLS + LANES))
+    level = jnp.broadcast_to(level[:, 0:1] + level[:, 1:2], (2 * ROWS, LANES))
 
     def forward(pair):
-        columns = jnp.concatenate([
-            jnp.concatenate([every_wide[pl.ds(q * 8 + chunk, 64, stride=16), :] for q in range(2)], axis=0)
-            for chunk in (2 * pair, 2 * pair + 1)
-        ], axis=1).astype(bf16)
-        value = dot(wide[...], jnp.concatenate([columns, columns], axis=0))
+        value = product(slice(pair * 256, (pair + 1) * 256))
         for side in range(2):
             here = slice((2 * pair + side) * LANES, (2 * pair + side + 1) * LANES)
-            partial[pair, :, side * LANES:(side + 1) * LANES] = (
-                value[:, side * LANES:(side + 1) * LANES] + mean[...] * own_sum[:, here]
-            )
-        half_sums(pair).start()
-
-    def finish(pair):
-        half_sums(pair).wait_recv()
-        for side in range(2):
-            chunk = 2 * pair + side
-            here = slice(side * LANES, (side + 1) * LANES)
-            found = partial[pair, mine, here] + from_sibling[pair, :, here]
-            rows = pl.ds(chunk, ROWS, stride=8)
-            rest = norm[rows, :] * (measured[rows, :] - found)
-            residual[rows, :] = rest
-            ratio[mine, chunk * LANES:(chunk + 1) * LANES] = rest.astype(bf16)
-        to_sibling(pair, mine).start()
+            found = value[:, side * LANES:(side + 1) * LANES] + level * own_sum[:, here]
+            rest = norm[:, here] * (measured[:, here] - found)
+            remainder[:, here] = rest
+            ratio[:, here] = rest.astype(bf16)
 
     def collect(pair):
-        to_sibling(pair, other).wait_recv()
         both = dot(weight[...], ratio[:, pair * 256:(pair + 1) * 256])
         value = both[:128] + both[128:]
-        for q in range(2):
-            for side in range(2):
-                straight[pl.ds(q * 8 + 2 * pair + side, 64, stride=16), :] = value[q * 64:(q + 1) * 64, side * LANES:(side + 1) * LANES]
-
-    for step in range(6):
-        if step < 4:
-            forward(step)
-        if 0 <= step - 1 < 4:
-            finish(step - 1)
-        if 0 <= step - 2 < 4:
-            collect(step - 2)
+        for step, number in enumerate(sequence):
+            low = first_slot(number, 0) * 16
+            for q in range(2):
+                line = step * 32 + q * 16
+                for side in range(2):
+                    straight[pl.ds(low + q * 8 + 2 * pair + side, 16, stride=16), :] = (
+                        value[line:line + 16, side * LANES:(side + 1) * LANES]
+                    )
+
+    for pair in range(4):
+        forward(pair)
+        collect(pair)
 
     arrival = (y % 2) * 32 + m
     for offset in OFFSETS:
@@ -299,6 +339,14 @@
         remote(linear.at[rows], arrived.at[slot(arrival)], out_send.at[0], out_recv.at[0], partner(offset)).start()
     arrived[slot(arrival)] = straight[slot(here_chip)].astype(bf16)
 
+    keep = [
+        pltpu.make_async_copy(
+            remainder.at[mine, pl.ds(chunk * LANES, LANES)], residual.at[:, chunk, :], load_sem.at[17 + chunk]
+        )
+        for chunk in range(8)
+    ]
+    for copy in keep:
+        copy.start()
     sine_row = sines(subset, lax.broadcasted_iota(jnp.int32, (8, LANES), 1) % ANGLES)[:1]
     for part in range(PARTS):
         cell = (lax.broadcasted_iota(jnp.int32, (block, LANES), 0) + part * block).astype(f32)
@@ -310,9 +358,13 @@
     arrived_all(every.at[slot(0, 63)], send_sem.at[0]).wait()
     arrived_all(every_aux.at[pl.ds(0, 63)], aux_send.at[0]).wait()
     for number in range(4):
-        half_sums(number).wait_send()
-        to_sibling(number, mine).wait_send()
-    load[2].wait()
+        near_rows(number, core).wait_send()
+        near_aux(number, core).wait_send()
+    for number in range(2):
+        near_input(number, mine).wait_send()
+    load_scale.wait()
+    for copy in keep:
+        copy.wait()
 
     arrived_all(arrived.at[slot(0, 63)], out_recv.at[0]).wait()
     back[...] = arrived[...]
@@ -353,28 +405,27 @@
     vmem = pl.BlockSpec(memory_space=pltpu.VMEM)
     hbm = pl.BlockSpec(memory_space=pltpu.HBM)
     dma = pltpu.SemaphoreType.DMA
-    lines = ROWS * 8
     back, residual, volume_near, scale_near, moved, depth = pl.pallas_call(
         main_kernel,
         in_specs=[hbm] * 8,
-        out_specs=(vmem,) * 6,
+        out_specs=(vmem, hbm, vmem, vmem, vmem, vmem),
         out_shape=(
-            jax.ShapeDtypeStruct((1024, LANES), bf16), jax.ShapeDtypeStruct((lines, LANES), f32),
+            jax.ShapeDtypeStruct((1024, LANES), bf16), jax.ShapeDtypeStruct((ROWS, 8, LANES), f32),
             jax.ShapeDtypeStruct(volume.shape, f32), jax.ShapeDtypeStruct(volume.shape, f32),
             jax.ShapeDtypeStruct((ANGLES, LANES), f32), jax.ShapeDtypeStruct((DEPTH, LANES), bf16),
         ),
         scratch_shapes=[
             pltpu.SMEM((ANGLES,), jnp.int32), pltpu.VMEM((ANGLES, 4 * ANGLES), jnp.int32),
             pltpu.VMEM((6, LANES), jnp.int32), pltpu.VMEM((2, FOOT, ANGLES), f32),
-            pltpu.VMEM((lines, LANES), f32), pltpu.VMEM((lines, LANES), f32),
+            pltpu.VMEM((2 * ROWS, CELLS), f32), pltpu.VMEM((2 * ROWS, CELLS), f32),
             pltpu.VMEM((ANGLES, CELLS), f32), pltpu.VMEM((1024, LANES), f32), pltpu.VMEM((512, LANES), bf16),
-            pltpu.VMEM((ANGLES, 1, LANES), f32), pltpu.VMEM((1024, LANES), bf16), pltpu.VMEM((64, 1, LANES), f32),
-            pltpu.VMEM((1024, LANES), f32), pltpu.VMEM((128, 2 * ROWS), f32), pltpu.VMEM((256, 2 * ROWS), bf16),
-            pltpu.VMEM((2 * ROWS, 256), bf16), pltpu.VMEM((2 * ROWS, LANES), f32), pltpu.VMEM((2 * ROWS, CELLS), bf16),
-            pltpu.VMEM((4, 2 * ROWS, 256), f32), pltpu.VMEM((4, ROWS, 256), f32),
+            pltpu.VMEM((ANGLES, 1, LANES), f32), pltpu.VMEM((2048, LANES), bf16), pltpu.VMEM((128, 1, LANES), f32),
+            pltpu.VMEM((256, LANES), f32), pltpu.VMEM((256, 2 * ROWS), f32), pltpu.VMEM((256, 2 * ROWS), bf16),
+            pltpu.VMEM((2 * ROWS, 512), bf16), pltpu.VMEM((256, CELLS + LANES), bf16),
+            pltpu.VMEM((2 * ROWS, CELLS), f32), pltpu.VMEM((2 * ROWS, CELLS), bf16),
             pltpu.VMEM((1024, LANES), bf16), pltpu.VMEM((1024, LANES), bf16),
-            dma((2 * PARTS,)), dma((4,)), dma((3,)), dma((1,)), dma((4,)), dma((1,)), dma((4,)),
-            dma((4,)), dma((4,)), dma((4,)), dma((4,)), dma((1,)), dma((1,)),
+            dma((2 * PARTS,)), dma((4,)), dma((25,)), dma((1,)), dma((4,)), dma((1,)), dma((4,)),
+            dma((4,)), dma((4,)), dma((4,)), dma((4,)), dma((2,)), dma((2,)), dma((1,)), dma((1,)),
         ],
         compiler_params=pltpu.CompilerParams(collective_id=0, has_side_effects=True, vmem_limit_bytes=28 << 20),
         cost_estimate=pl.CostEstimate(flops=10 ** 9, bytes_accessed=100 << 20, transcendentals=0),
@@ -382,14 +433,14 @@
     )(
         *[pltpu.with_memory_space_constraint(array, pltpu.HBM) for array in (
             subset, row_start, row_order.reshape(6, LANES), jnp.transpose(axial_weights, (0, 2, 1)), volume, voxel_norm,
-            measured.reshape(lines, LANES), ray_norm.reshape(lines, LANES),
+            measured.reshape(ROWS, 8, LANES), ray_norm.reshape(ROWS, 8, LANES),
         )]
     )
     new_volume, residual = pl.pallas_call(
         final_kernel,
         in_specs=[vmem, vmem, vmem, vmem, vmem, pl.BlockSpec(memory_space=pl.ANY)],
         out_specs=(hbm, hbm),
-        out_shape=(jax.ShapeDtypeStruct(volume.shape, f32), jax.ShapeDtypeStruct((lines, LANES), f32)),
+        out_shape=(jax.ShapeDtypeStruct(volume.shape, f32), jax.ShapeDtypeStruct((ROWS, 8, LANES), f32)),
         scratch_shapes=[
             pltpu.VMEM((512, LANES), f32), pltpu.VMEM((2, LANES, COLS), bf16), pltpu.VMEM(volume.shape, f32),
             dma((2 * PARTS,)), dma,

time: 33.8 us -> 32.6 us (0.964); the launches traced: 33.3 us -> 32.4 us
  Pallas kernels: 32.6 us -> 31.8 us
    pallas_call x1, Pallas kernels: 29.4 us -> 28.6 us  [shards(): pl.pallas_call(main_kernel, in_specs=[hbm] * 8, out_specs=(vmem, hbm, vme...]
where the time goes in v7:
time: 32.6 us; the launch traced here: 32.4 us
  Pallas kernels  31.8 us (98%)
  between operations  0.64 us (2%)
    pallas_call x1, Pallas kernels, shards(): pl.pallas_call(main_kernel, in_specs=[hbm] * 8, out_specs=(vmem, hbm, vme...  28.6 us
    pallas_call x1, Pallas kernels, shards(): pl.pallas_call(final_kernel, in_specs=[vmem, vmem, vmem, vmem, vmem, pl.B...  3.2 us

profile of v7, /device:TPU:1, one launch (start us, length us, event | category | flops | bytes accessed | tf_op | source)
XLA Modules:
  0.0 32.4 jit_solution(18391498111195753839)
XLA Ops:
  0.6 28.6 %exchange.1 = (bf16[1024,128]{1,0:T(8,128)(2,1)S(1)}, f32[192,8,128]{2,1,0:T(8,128)S(1)}, f32[2,768,768]{2,1,0:T(8,128)S(1)}, f32[2,768,768]{2,1,0:T(8,128)S(1)}...) custom-call(s32[32]{0:T(128)} %subset_hbm.1, s32[32,128]{1,0:T(8,128)} %row_start_hbm.1, s32[6,128]{1,0:T(8,128)} %bitcast.8, ...), custom_call_target="tpu_custom_call" | custom-call | flops 1000000000 | bytes 104857600 | tf_op jit(solution)/shard_map/exchange/pallas_call | solution.py:408
  29.2 3.2 %final.1 = (f32[2,768,768]{2,1,0:T(8,128)}, f32[192,8,128]{2,1,0:T(8,128)}) custom-call(f32[32,128]{1,0:T(8,128)S(1)} %get-tuple-element.10.moved, bf16[768,128]{1,0:T(8,128)(2,1)S(1)} %get-tuple-element.11.depth, bf16[1024,128]{1,0:T(8,128)(2,1)S(1)} %get-tuple-element.12.back, f32[2,768,768]{2,1,0:T(8,128)S(1)} %get-tuple-element.13.volume, ...), custom_call_target="tpu_custom_call" | custom-call | flops 226492416 | bytes 14155776 | tf_op jit(solution)/shard_map/final/pallas_call | solution.py:439

commit v8 on v7

--- a/solution.py
+++ b/solution.py
@@ -18,6 +18,7 @@
 CELLS = 1024
 ROWS = 192
 PARTS = 3
+OUT_PARTS = 6
 OFFSETS = sorted(
     itertools.product(range(4), repeat=3), key=lambda offset: -sum(min(step, 4 - step) for step in offset)
 )[:-1]
@@ -247,13 +248,17 @@
     def place(step, number, side, turn):
         low = first_slot(number, side)
         table = every_aux[pl.ds(low, 16)].reshape(16, LANES)
-        offset = rows - table[:, 16:17]
+        offset = (rows - table[:, 16:17]).astype(jnp.int32)
+        inside, entry = (offset >= 0) & (offset < FOOT), offset & (FOOT - 1)
         lane = lax.broadcasted_iota(jnp.int32, (16, LANES), 1)
         every_wide[...] = every[slot(low, 16), :].astype(f32)
         for q in range(2):
-            value = jnp.zeros_like(offset)
-            for r in range(FOOT):
-                value = jnp.where(offset == float(r), table[:, q * FOOT + r:q * FOOT + r + 1], value)
+            value = jnp.where(inside, jnp.concatenate([
+                jnp.take_along_axis(
+                    table, entry[:, part * LANES:(part + 1) * LANES] + q * FOOT, axis=1, mode="promise_in_bounds"
+                )
+                for part in range(3)
+            ], axis=1), 0.0)
             line = step * 64 + turn * 32 + q * 16
             tall[line:line + 16, :] = value
             if turn == 0:
@@ -373,7 +378,7 @@
 
 def final_kernel(moved, depth, back, volume, scale, residual_in, new_volume, residual, straight, spread, staged, sems, rest_sem):
     f32 = jnp.float32
-    block = DEPTH // PARTS
+    block = DEPTH // OUT_PARTS
     keep = pltpu.make_async_copy(residual_in, residual, rest_sem)
     keep.start()
     straight[...] = back[:512].astype(f32) + back[512:].astype(f32)
@@ -388,12 +393,12 @@
             spread[q, ANGLES:2 * ANGLES, here] = low
             spread[q, 2 * ANGLES:3 * ANGLES, here] = high
             spread[q, 3 * ANGLES:4 * ANGLES, here] = jnp.zeros_like(high)
-        for part in range(PARTS):
+        for part in range(OUT_PARTS):
             here = slice(part * block, (part + 1) * block)
             update = dot(depth[here, :], spread[q])
             staged[q, here, :] = jnp.maximum(0.0, volume[q, here, :] + scale[q, here, :] * update)
             rows = pl.ds(part * block, block)
-            copies.append(pltpu.make_async_copy(staged.at[q, rows], new_volume.at[q, rows], sems.at[q * PARTS + part]))
+            copies.append(pltpu.make_async_copy(staged.at[q, rows], new_volume.at[q, rows], sems.at[q * OUT_PARTS + part]))
             copies[-1].start()
     for copy in copies:
         copy.wait()
@@ -443,7 +448,7 @@
         out_shape=(jax.ShapeDtypeStruct(volume.shape, f32), jax.ShapeDtypeStruct((ROWS, 8, LANES), f32)),
         scratch_shapes=[
             pltpu.VMEM((512, LANES), f32), pltpu.VMEM((2, LANES, COLS), bf16), pltpu.VMEM(volume.shape, f32),
-            dma((2 * PARTS,)), dma,
+            dma((2 * OUT_PARTS,)), dma,
         ],
         compiler_params=pltpu.CompilerParams(vmem_limit_bytes=28 << 20),
         cost_estimate=pl.CostEstimate(flops=6 * 64 * DEPTH * COLS, bytes_accessed=4 * 6 * DEPTH * COLS, transcendentals=0),

time: 32.6 us -> 31.3 us (0.960)
  Pallas kernels: 31.8 us -> 30.5 us
    pallas_call x1, Pallas kernels: 28.6 us -> 27.6 us  [shards(): pl.pallas_call(main_kernel, in_specs=[hbm] * 8, out_specs=(vmem, hbm, vme...]
where the time goes in v8:
time: 31.3 us; the launch traced here: 31.2 us
  Pallas kernels  30.5 us (97%)
  between operations  0.64 us (2%)
    pallas_call x1, Pallas kernels, shards(): pl.pallas_call(main_kernel, in_specs=[hbm] * 8, out_specs=(vmem, hbm, vme...  27.6 us
    pallas_call x1, Pallas kernels, shards(): pl.pallas_call(final_kernel, in_specs=[vmem, vmem, vmem, vmem, vmem, pl.B...  2.94 us

profile of v8, /device:TPU:1, one launch (start us, length us, event | category | flops | bytes accessed | tf_op | source)
XLA Modules:
  0.0 31.2 jit_solution(1462687890515387913)
XLA Ops:
  0.6 27.6 %exchange.1 = (bf16[1024,128]{1,0:T(8,128)(2,1)S(1)}, f32[192,8,128]{2,1,0:T(8,128)S(1)}, f32[2,768,768]{2,1,0:T(8,128)S(1)}, f32[2,768,768]{2,1,0:T(8,128)S(1)}...) custom-call(s32[32]{0:T(128)} %subset_hbm.1, s32[32,128]{1,0:T(8,128)} %row_start_hbm.1, s32[6,128]{1,0:T(8,128)} %bitcast.8, ...), custom_call_target="tpu_custom_call" | custom-call | flops 1000000000 | bytes 104857600 | tf_op jit(solution)/shard_map/exchange/pallas_call | solution.py:413
  28.2 2.9 %final.1 = (f32[2,768,768]{2,1,0:T(8,128)}, f32[192,8,128]{2,1,0:T(8,128)}) custom-call(f32[32,128]{1,0:T(8,128)S(1)} %get-tuple-element.10.moved, bf16[768,128]{1,0:T(8,128)(2,1)S(1)} %get-tuple-element.11.depth, bf16[1024,128]{1,0:T(8,128)(2,1)S(1)} %get-tuple-element.12.back, f32[2,768,768]{2,1,0:T(8,128)S(1)} %get-tuple-element.13.volume, ...), custom_call_target="tpu_custom_call" | custom-call | flops 226492416 | bytes 14155776 | tf_op jit(solution)/shard_map/final/pallas_call | solution.py:444

commit v9 on v8

--- a/solution.py
+++ b/solution.py
@@ -288,8 +288,22 @@
 
     def turn_over(part):
         high, low = halves(tall[part * LANES:(part + 1) * LANES, :].T)
-        wide[:, part * LANES:(part + 1) * LANES] = high
-        wide[:, 256 + part * LANES:256 + (part + 1) * LANES] = low
+        wide[part, :, 0:LANES] = high
+        wide[part, :, LANES:2 * LANES] = low
+
+    def product(part, here):
+        right = matrix[part * LANES:(part + 1) * LANES, here]
+        return dot(wide[part], jnp.concatenate([right, right], axis=0))
+
+    def level_of(part):
+        value = product(part, slice(CELLS, CELLS + LANES))
+        return jnp.broadcast_to(value[:, 0:1] + value[:, 1:2], (2 * ROWS, LANES))
+
+    def sums(part, pair, level):
+        value = product(part, slice(pair * 256, (pair + 1) * 256))
+        for side in range(2):
+            here = slice((2 * pair + side) * LANES, (2 * pair + side + 1) * LANES)
+            yield here, value[:, side * LANES:(side + 1) * LANES] + level * own_sum[:, here]
 
     sequence = (0, 1, 3, 2)
     own_rows(0, 0)
@@ -301,22 +315,19 @@
     near_input(0, other).wait_recv()
     near_input(1, other).wait_recv()
     own_rows(3, 2)
+    near_input(0, mine).wait_send()
+    level = level_of(0)
+    for pair in range(4):
+        for here, found in sums(0, pair, level):
+            measured[:, here] = measured[:, here] - found
     sibling_rows(2, 3)
     sibling_rows(3, 2)
     turn_over(1)
 
-    def product(here):
-        right = matrix[:, here]
-        return dot(wide[...], jnp.concatenate([right, right], axis=0))
-
-    level = product(slice(CELLS, CELLS + LANES))
-    level = jnp.broadcast_to(level[:, 0:1] + level[:, 1:2], (2 * ROWS, LANES))
+    level = level_of(1)
 
     def forward(pair):
-        value = product(slice(pair * 256, (pair + 1) * 256))
-        for side in range(2):
-            here = slice((2 * pair + side) * LANES, (2 * pair + side + 1) * LANES)
-            found = value[:, side * LANES:(side + 1) * LANES] + level * own_sum[:, here]
+        for here, found in sums(1, pair, level):
             rest = norm[:, here] * (measured[:, here] - found)
             remainder[:, here] = rest
             ratio[:, here] = rest.astype(bf16)
@@ -365,8 +376,7 @@
     for number in range(4):
         near_rows(number, core).wait_send()
         near_aux(number, core).wait_send()
-    for number in range(2):
-        near_input(number, mine).wait_send()
+    near_input(1, mine).wait_send()
     load_scale.wait()
     for copy in keep:
         copy.wait()
@@ -426,7 +436,7 @@
             pltpu.VMEM((ANGLES, CELLS), f32), pltpu.VMEM((1024, LANES), f32), pltpu.VMEM((512, LANES), bf16),
             pltpu.VMEM((ANGLES, 1, LANES), f32), pltpu.VMEM((2048, LANES), bf16), pltpu.VMEM((128, 1, LANES), f32),
             pltpu.VMEM((256, LANES), f32), pltpu.VMEM((256, 2 * ROWS), f32), pltpu.VMEM((256, 2 * ROWS), bf16),
-            pltpu.VMEM((2 * ROWS, 512), bf16), pltpu.VMEM((256, CELLS + LANES), bf16),
+            pltpu.VMEM((2, 2 * ROWS, 256), bf16), pltpu.VMEM((256, CELLS + LANES), bf16),
             pltpu.VMEM((2 * ROWS, CELLS), f32), pltpu.VMEM((2 * ROWS, CELLS), bf16),
             pltpu.VMEM((1024, LANES), bf16), pltpu.VMEM((1024, LANES), bf16),
             dma((2 * PARTS,)), dma((4,)), dma((25,)), dma((1,)), dma((4,)), dma((1,)), dma((4,)),

time: 31.3 us -> 31.1 us (level)
  no operation moved by 1% of the time
where the time goes in v9:
time: 31.1 us; the launch traced here: 31 us
  Pallas kernels  30.3 us (97%)
  between operations  0.64 us (2%)
    pallas_call x1, Pallas kernels, shards(): pl.pallas_call(main_kernel, in_specs=[hbm] * 8, out_specs=(vmem, hbm, vme...  27.4 us
    pallas_call x1, Pallas kernels, shards(): pl.pallas_call(final_kernel, in_specs=[vmem, vmem, vmem, vmem, vmem, pl.B...  2.94 us

profile of v9, /device:TPU:1, one launch (start us, length us, event | category | flops | bytes accessed | tf_op | source)
XLA Modules:
  0.0 31.0 jit_solution(12634872755463606977)
XLA Ops:
  0.6 27.4 %exchange.1 = (bf16[1024,128]{1,0:T(8,128)(2,1)S(1)}, f32[192,8,128]{2,1,0:T(8,128)S(1)}, f32[2,768,768]{2,1,0:T(8,128)S(1)}, f32[2,768,768]{2,1,0:T(8,128)S(1)}...) custom-call(s32[32]{0:T(128)} %subset_hbm.1, s32[32,128]{1,0:T(8,128)} %row_start_hbm.1, s32[6,128]{1,0:T(8,128)} %bitcast.8, ...), custom_call_target="tpu_custom_call" | custom-call | flops 1000000000 | bytes 104857600 | tf_op jit(solution)/shard_map/exchange/pallas_call | solution.py:423
  28.0 2.9 %final.1 = (f32[2,768,768]{2,1,0:T(8,128)}, f32[192,8,128]{2,1,0:T(8,128)}) custom-call(f32[32,128]{1,0:T(8,128)S(1)} %get-tuple-element.10.moved, bf16[768,128]{1,0:T(8,128)(2,1)S(1)} %get-tuple-element.11.depth, bf16[1024,128]{1,0:T(8,128)(2,1)S(1)} %get-tuple-element.12.back, f32[2,768,768]{2,1,0:T(8,128)S(1)} %get-tuple-element.13.volume, ...), custom_call_target="tpu_custom_call" | custom-call | flops 226492416 | bytes 14155776 | tf_op jit(solution)/shard_map/final/pallas_call | solution.py:454

commit v10 on v9

--- a/solution.py
+++ b/solution.py
@@ -279,7 +279,8 @@
         near_aux(number, core).start()
         arrived_all(every.at[slot(low, count)], recv_sem.at[number]).wait()
         near_rows(number, core).start()
-        place(step, number, core, 0)
+        if step < 3:
+            place(step, number, core, 0)
 
     def sibling_rows(step, number):
         near_aux(number, 1 - core).wait_recv()
@@ -312,10 +313,11 @@
     own_rows(2, 3)
     sibling_rows(1, 1)
     turn_over(0)
+    own_rows(3, 2)
+    near_input(0, mine).wait_send()
     near_input(0, other).wait_recv()
     near_input(1, other).wait_recv()
-    own_rows(3, 2)
-    near_input(0, mine).wait_send()
+    place(3, 2, core, 0)
     level = level_of(0)
     for pair in range(4):
         for here, found in sums(0, pair, level):

time: 31.1 us -> 31 us (level)
  no operation moved by 1% of the time
where the time goes in v10:
time: 31 us; the launch traced here: 30.9 us
  Pallas kernels  30.2 us (97%)
  between operations  0.64 us (2%)
    pallas_call x1, Pallas kernels, shards(): pl.pallas_call(main_kernel, in_specs=[hbm] * 8, out_specs=(vmem, hbm, vme...  27.3 us
    pallas_call x1, Pallas kernels, shards(): pl.pallas_call(final_kernel, in_specs=[vmem, vmem, vmem, vmem, vmem, pl.B...  2.94 us

profile of v10, /device:TPU:1, one launch (start us, length us, event | category | flops | bytes accessed | tf_op | source)
XLA Modules:
  0.0 30.9 jit_solution(2817225750108345366)
XLA Ops:
  0.6 27.3 %exchange.1 = (bf16[1024,128]{1,0:T(8,128)(2,1)S(1)}, f32[192,8,128]{2,1,0:T(8,128)S(1)}, f32[2,768,768]{2,1,0:T(8,128)S(1)}, f32[2,768,768]{2,1,0:T(8,128)S(1)}...) custom-call(s32[32]{0:T(128)} %subset_hbm.1, s32[32,128]{1,0:T(8,128)} %row_start_hbm.1, s32[6,128]{1,0:T(8,128)} %bitcast.8, ...), custom_call_target="tpu_custom_call" | custom-call | flops 1000000000 | bytes 104857600 | tf_op jit(solution)/shard_map/exchange/pallas_call | solution.py:425
  27.9 2.9 %final.1 = (f32[2,768,768]{2,1,0:T(8,128)}, f32[192,8,128]{2,1,0:T(8,128)}) custom-call(f32[32,128]{1,0:T(8,128)S(1)} %get-tuple-element.10.moved, bf16[768,128]{1,0:T(8,128)(2,1)S(1)} %get-tuple-element.11.depth, bf16[1024,128]{1,0:T(8,128)(2,1)S(1)} %get-tuple-element.12.back, f32[2,768,768]{2,1,0:T(8,128)S(1)} %get-tuple-element.13.volume, ...), custom_call_target="tpu_custom_call" | custom-call | flops 226492416 | bytes 14155776 | tf_op jit(solution)/shard_map/final/pallas_call | solution.py:456
